TPU v7x, 256 devices: a whole 4x4x8 slice. The times are simulated.
256 devices in a mesh: tile: 32 (over z, y), depth: 8 (over x, core).
Axes of the slice: x: 4, y: 4, z: 8, core: 2. Of those that a mesh axis runs over, the one named last changes fastest.
Arguments:
- phase: float32 [8, 32, 384, 384], P('depth', 'tile'), may hold values from -3.140625 to 3.140625
- absorb: float32 [8, 32, 384, 384], P('depth', 'tile'), may hold values from 0 to 0.3
- probe: float32 [2, 4, 128, 128], replicated, may hold values from -6 to 6
- row_offsets: int32 [32], replicated, may hold values from 0 to 2944
- col_offsets: int32 [32], replicated, may hold values from 0 to 1408
- tile_slot: int32 [32], replicated, may hold values from 0 to 31, each once
- counts: int32 [32, 128, 128], P('tile'), may hold values from 0 to 128
Outputs:
- phase_grad: float32 [8, 32, 384, 384], P('depth', 'tile')
- absorb_grad: float32 [8, 32, 384, 384], P('depth', 'tile')
Inputs may be any that keep to these rules, and one draw needn't show every extreme that they name: tile_slot names every storage index once.
All inputs are finite; a program needn't handle non-finite values.
Results may differ from a plain program's by a relative error of at most 0.0003.
Values sent between devices are 32-bit elements; how exact they have to be, the bound alone decides.
A program may use at most 128 MiB of HBM per device.

v0:
```python
import math

import jax
import jax.numpy as jnp
from jax import lax
from jax.sharding import PartitionSpec as P

W = 128
MODES = 4
GY = 4


count_scale = 0.0078125
loss_scale = 0.03125
fresnel_strength = 40.0


def shifted(value, axis, steps):
    count = lax.axis_size(axis)
    first, last = (max(0, -steps), min(count, count - steps))
    return lax.ppermute(value, axis, [(source, source + steps) for source in range(first, last)])


def dft_tables(extent):
    indices = jnp.arange(extent, dtype=jnp.int32)
    phase_steps = indices[:, None] * indices[None, :] % extent
    angles = phase_steps.astype(jnp.float32) * (2.0 * math.pi / extent)
    factor = 1.0 / math.sqrt(extent)
    return (jnp.cos(angles) * factor, -jnp.sin(angles) * factor)


def fresnel(extent):
    indices = jnp.arange(extent, dtype=jnp.int32)
    signed = ((indices + extent // 2) % extent - extent // 2).astype(jnp.float32) / extent
    chirps = fresnel_strength * (signed[:, None] ** 2 + signed[None, :] ** 2)
    return jnp.stack([jnp.cos(chirps), -jnp.sin(chirps)])


def transform(wave_field, cos_t, sin_t):
    extent = cos_t.shape[0]
    right_table = jnp.concatenate(
        [jnp.concatenate([cos_t, sin_t], 1), jnp.concatenate([-sin_t, cos_t], 1)], 0
    )
    joined = jnp.concatenate([wave_field[0], wave_field[1]], -1)
    half_done = jnp.einsum("...ij,jk->...ik", joined, right_table, precision=lax.Precision.HIGHEST)
    cos_part = jnp.einsum("ij,...jk->...ik", cos_t, half_done, precision=lax.Precision.HIGHEST)
    sin_part = jnp.einsum("ij,...jk->...ik", sin_t, half_done, precision=lax.Precision.HIGHEST)
    real_out = cos_part[..., :extent] - sin_part[..., extent:]
    imag_out = cos_part[..., extent:] + sin_part[..., :extent]
    return jnp.stack([real_out, imag_out])


def times_complex(left_op, right_op):
    return jnp.stack(
        [
            left_op[0] * right_op[0] - left_op[1] * right_op[1],
            left_op[0] * right_op[1] + left_op[1] * right_op[0],
        ]
    )


def conj_times(left_op, right_op):
    return jnp.stack(
        [
            left_op[0] * right_op[0] + left_op[1] * right_op[1],
            left_op[0] * right_op[1] - left_op[1] * right_op[0],
        ]
    )


def propagate(wave_field, tables):
    cos_t, sin_t, kernel = tables
    spectrum = transform(wave_field, cos_t, sin_t)
    return transform(times_complex(kernel, spectrum), cos_t, -sin_t)


def adjoint(wave_field, tables):
    cos_t, sin_t, kernel = tables
    spectrum = transform(wave_field, cos_t, sin_t)
    return transform(conj_times(kernel, spectrum), cos_t, -sin_t)


def section(wave_field, trans, tables):
    wave_field = propagate(times_complex(trans[:, :, 0, None], wave_field), tables)
    return wave_field


def section_back(wave_field, gradient, trans, tables):
    layer_total = trans.shape[2]
    layer_no = 0
    inputs = [wave_field]
    pieces = [None] * layer_total
    for layer_no in reversed(range(layer_total)):
        arriving = adjoint(gradient, tables)
        pieces[layer_no] = jnp.sum(conj_times(inputs[layer_no], arriving), axis=2)
        gradient = conj_times(trans[:, :, layer_no, None], arriving)
    return (gradient, jnp.stack(pieces, 2))


def exit_gradient(exit_field, counts, cos_t, sin_t):
    far_field = transform(exit_field, cos_t, sin_t)
    intensity = jnp.sum(far_field[0] ** 2 + far_field[1] ** 2, axis=1)
    residual = intensity - count_scale * counts.astype(jnp.float32)
    back_field = 4.0 * loss_scale * residual[None, :, None] * far_field
    return transform(back_field, cos_t, -sin_t)


def take_group(stacked, group_slot):
    return lax.dynamic_index_in_dim(stacked, group_slot, 0, keepdims=False)


def relay_chain(trans, probe, counts, tables, my_segment, depth_count):
    cos_t, sin_t, kernel = tables
    pos_count = counts.shape[0]
    groups = 1
    group_modes = MODES // groups
    starts = probe.reshape(2, groups, group_modes, W, W).transpose(1, 0, 2, 3, 4)[:, :, None]
    step_total = depth_count + groups - 1
    last_segment = depth_count - 1

    def forward_step(step_no, loop_state):
        incoming, stored, exit_waves = loop_state
        group_no = step_no - my_segment
        is_live = (group_no >= 0) & (group_no < groups)
        group_slot = jnp.clip(group_no, 0, groups - 1)
        wave_in = jnp.where(my_segment == 0, take_group(starts, group_slot), incoming)
        kept_wave = take_group(stored, group_slot)
        stored = lax.dynamic_update_index_in_dim(
            stored, jnp.where(is_live, wave_in, kept_wave), group_slot, 0
        )
        wave_out = section(wave_in, trans, tables)
        kept_exit = take_group(exit_waves, group_slot)
        fresh_exit = jnp.where(is_live & (my_segment == last_segment), wave_out, kept_exit)
        exit_waves = lax.dynamic_update_index_in_dim(exit_waves, fresh_exit, group_slot, 0)
        incoming = shifted(wave_out, "depth", 1)
        return (incoming, stored, exit_waves)

    empty_groups = jnp.zeros_like(starts)
    first_state = (jnp.zeros_like(starts[0]), empty_groups, empty_groups)
    unused_wave, stored, exit_waves = lax.fori_loop(0, step_total, forward_step, first_state)
    exit_field = exit_waves.transpose(1, 2, 0, 3, 4, 5).reshape(2, pos_count, MODES, W, W)
    exit_grad = exit_gradient(exit_field, counts, cos_t, sin_t)
    exit_grads = exit_grad.reshape(2, pos_count, groups, group_modes, W, W).transpose(
        2, 0, 1, 3, 4, 5
    )

    def backward_step(step_no, loop_state):
        incoming, grad_sum = loop_state
        group_no = step_no - (last_segment - my_segment)
        is_live = (group_no >= 0) & (group_no < groups)
        group_slot = jnp.clip(group_no, 0, groups - 1)
        grad_in = jnp.where(
            my_segment == last_segment, take_group(exit_grads, group_slot), incoming
        )
        grad_out, object_grad = section_back(take_group(stored, group_slot), grad_in, trans, tables)
        grad_sum = grad_sum + jnp.where(is_live, object_grad, 0.0)
        incoming = shifted(grad_out, "depth", -1)
        return (incoming, grad_sum)

    back_state = (jnp.zeros_like(starts[0]), jnp.zeros_like(trans))
    unused_grad, object_grad = lax.fori_loop(0, step_total, backward_step, back_state)
    return object_grad


def local(phase, absorb, probe, row_offsets, col_offsets, tile_slot, counts):
    depth_count = lax.axis_size("depth")
    my_tile = lax.axis_index("tile")
    my_segment = lax.axis_index("depth")
    slice_count = phase.shape[0]
    tile_side = phase.shape[2]
    cos_t, sin_t = dft_tables(W)
    tables = (cos_t, sin_t, fresnel(W))
    grid_place = jnp.sum(
        jnp.where(tile_slot == my_tile, jnp.arange(tile_slot.shape[0], dtype=jnp.int32), 0)
    )
    tile_top = grid_place // GY * tile_side
    tile_left = grid_place % GY * tile_side
    padded = jnp.pad(jnp.stack([phase[:, 0], absorb[:, 0]]), ((0, 0), (0, 0), (W, W), (W, W)))
    zero_idx = jnp.zeros((), jnp.int32)

    def corner(row_start, col_start):
        top_edge = jnp.clip(row_start - tile_top + W, 0, tile_side + W)
        left_edge = jnp.clip(col_start - tile_left + W, 0, tile_side + W)
        return (top_edge, left_edge)

    def extract(row_start, col_start):
        top_edge, left_edge = corner(row_start, col_start)
        return lax.dynamic_slice(
            padded, (zero_idx, zero_idx, top_edge, left_edge), (2, slice_count, W, W)
        )

    windows = lax.psum_scatter(
        jax.vmap(extract)(row_offsets, col_offsets), "tile", scatter_dimension=0, tiled=True
    )
    damping = jnp.exp(-windows[:, 1])
    trans = jnp.stack([damping * jnp.cos(windows[:, 0]), damping * jnp.sin(windows[:, 0])])
    object_grad = relay_chain(trans, probe, counts, tables, my_segment, depth_count)
    phase_part = trans[0] * object_grad[1] - trans[1] * object_grad[0]
    absorb_part = -(trans[0] * object_grad[0] + trans[1] * object_grad[1])
    window_grads = jnp.stack([phase_part, absorb_part], 1)
    empty_tile = jnp.zeros((2, slice_count, tile_side + 2 * W, tile_side + 2 * W), jnp.float32)
    part_rows = lax.all_gather(window_grads, "tile", axis=0, tiled=True)

    def add_one(item_no, running):
        row_start = lax.dynamic_index_in_dim(row_offsets, item_no, 0, keepdims=False)
        col_start = lax.dynamic_index_in_dim(col_offsets, item_no, 0, keepdims=False)
        top_edge, left_edge = corner(row_start, col_start)
        where_at = (zero_idx, zero_idx, top_edge, left_edge)
        current = lax.dynamic_slice(running, where_at, (2, slice_count, W, W))
        addend = lax.dynamic_index_in_dim(part_rows, item_no, 0, keepdims=False)
        return lax.dynamic_update_slice(running, current + addend, where_at)

    deposit_sum = lax.fori_loop(0, part_rows.shape[0], add_one, empty_tile)
    interior = deposit_sum[:, :, W : W + tile_side, W : W + tile_side]
    return (interior[0][:, None], interior[1][:, None])


def solution(mesh):
    in_specs = (
        P("depth", "tile", None, None),
        P("depth", "tile", None, None),
        P(),
        P(),
        P(),
        P(),
        P("tile", None, None),
    )
    out_specs = (P("depth", "tile", None, None), P("depth", "tile", None, None))
    return jax.shard_map(local, mesh=mesh, in_specs=in_specs, out_specs=out_specs, check_vma=False)
```

profile of v0, /device:TPU:2, one launch (start us, length us, event | category | flops | bytes accessed | tf_op | source)
XLA Modules:
  0.0 863.8 jit_solution(3031696277451205585)
XLA Ops:
  12.8 84.3 %while.59 = (s32[]{:T(128)}, f32[2,1,640,640]{3,2,1,0:T(8,128)S(1)}, s32[32,4]{0,1:T(4,128)S(1)}, f32[32,2,1,128,128]{4,3,1,2,0:T(8,128)}, s32[]{:T(128)}) while((s32[]{:T(128)}, f32[2,1,640,640]{3,2,1,0:T(8,128)S(1)}, s32[32,4]{0,1:T(4,128)S(1)}, f32[32,2,1,128,128]{4,3,1,2,0:T(8,128)}, s32[]{:T(128)}) %tuple.181), condition=%wide.while_cond, body=%wide.while_body.sunk | while | flops 2 | bytes 263793 | solution.py:188
  97.9 223.7 %reduce-scatter.2.cloned.1.call-done = f32[1,2,1,128,128]{4,3,2,1,0:T(8,128)} async-done(((f32[32,2,1,128,128]{4,3,2,1,0:T(8,128)}), f32[1,2,1,128,128]{4,3,2,1,0:T(8,128)}) %reduce-scatter.2.cloned.1.call-update) | async-done | bytes 131088 | tf_op jit(solution)/shard_map/reduce_scatter | solution.py:192
  322.8 146.1 %while.60 = (s32[]{:T(128)}, f32[2,1,4,128,128]{3,4,2,1,0:T(8,128)S(1)}, f32[1,2,1,4,128,128]{5,4,3,1,2,0:T(8,128)S(1)}, f32[1,2,1,4,128,128]{4,5,3,2,1,0:T(8,12...) while((s32[]{:T(128)}, ...), condition=%wide.region_3.4_spmd.clone.clone.clone.clone, body=%wide.region_2.3_spmd.clone.clone.clone.clone.sunk | while | flops 1613791232 | bytes 20316904 | solution.py:140
  332.5 8.6 collective-permute-done
  350.7 8.6 collective-permute-done
  369.0 8.6 collective-permute-done
  387.3 8.6 collective-permute-done
  405.5 8.6 collective-permute-done
  423.8 8.6 collective-permute-done
  442.0 8.6 collective-permute-done
  460.3 8.6 collective-permute-done
  474.7 135.1 %while.61 = (s32[]{:T(128)}, f32[2,1,4,128,128]{3,4,2,1,0:T(8,128)S(1)}, f32[2,1,1,128,128]{3,4,0,2,1:T(8,128)S(1)}, f32[1,1,128,128]{2,3,1,0:T(8,128)S(1)}, pre...) while((s32[]{:T(128)}, ...), condition=%wide.region_7.8_spmd.clone.clone.clone.clone, body=%wide.region_5.7_spmd.clone.clone.clone.clone.sunk | while | flops 1613987840 | bytes 20841176 | solution.py:161
  483.3 6.9 collective-permute-done.1
  500.4 6.9 collective-permute-done.1
  513.7 3.7 collective-permute-start.1
  517.5 6.9 collective-permute-done.1
  534.6 6.9 collective-permute-done.1
  551.7 6.9 collective-permute-done.1
  568.8 6.9 collective-permute-done.1
  582.1 3.7 collective-permute-start.1
  585.9 6.9 collective-permute-done.1
  602.9 6.9 collective-permute-done.1
  610.9 81.1 %all-gather.2.cloned.1.call-done = f32[32,2,1,128,128]{4,3,2,1,0:T(8,128)} async-done(((f32[1,2,1,128,128]{4,3,2,1,0:T(8,128)}), f32[32,2,1,128,128]{4,3,2,1,0:T(8,128)}) %all-gather.2.cloned.1.call-update) | async-done | bytes 4194320 | tf_op jit(solution)/shard_map/all_gather | solution.py:202
  692.2 163.7 %while.58 = (s32[]{:T(128)}, f32[2,1,640,640]{3,2,1,0:T(8,128)S(1)}, s32[32]{0:T(128)S(1)}, s32[]{:T(128)}, s32[32]{0:T(128)S(1)}, /*index=5*/s32[]{:T(128)}, f3...) while((s32[]{:T(128)}, f32[2,1,640,640]{3,2,1,0:T(8,128)S(1)}, ...), condition=%wide.region_9.10_spmd, body=%wide.region_8.9_spmd.sunk | while | flops 32778 | bytes 655605 | solution.py:213
  (531 shorter events, 365.4 us)
Async XLA Ops:
  7.2 5.5 copy-start.2
  7.2 5.5 copy-start.3
  7.2 314.4 %reduce-scatter.2.cloned.1.call-start = ((), (), s32[]{:S(2)}) async-start(), calls=%async_computation.1 | async-start | bytes 4325376 | tf_op jit(solution)/shard_map/reduce_scatter | solution.py:192
  12.7 84.5 %copy-start.1 = (s32[1,128,128]{2,1,0:T(8,128)S(1)}, s32[1,128,128]{2,1,0:T(8,128)}, u32[]{:S(2)}) copy-start(s32[1,128,128]{2,1,0:T(8,128)} %param.19) | copy-start | bytes 196612
  97.1 594.9 %all-gather.2.cloned.1.call-start = ((), (), s32[]{:S(2)}) async-start(), calls=%async_computation.2 | async-start | bytes 4325376 | tf_op jit(solution)/shard_map/all_gather | solution.py:202
  330.4 10.7 %collective-permute-start = (f32[2,1,4,128,128]{3,4,2,1,0:T(8,128)}, f32[2,1,4,128,128]{3,4,2,1,0:T(8,128)S(1)}, u32[]{:S(2)}, u32[]{:S(2)}) collective-permute-start(f32[2,1,4,128,128]{3,4,2,1,0:T(8,128)} %pad_maximum_fusion.9), channel_id=1, source_target_pairs={{0,1},{1,2},{2,3},{3,4},{4,5},{5,6},{6,7},{8,9},{9,10},{10,11},{11... | collective-permute-start | bytes 1572872 | tf_op jit(solution)/shard_map/while/body/eval_jaxpr/ppermute | solution.py:21
  348.6 10.7 %collective-permute-start = (f32[2,1,4,128,128]{3,4,2,1,0:T(8,128)}, f32[2,1,4,128,128]{3,4,2,1,0:T(8,128)S(1)}, u32[]{:S(2)}, u32[]{:S(2)}) collective-permute-start(f32[2,1,4,128,128]{3,4,2,1,0:T(8,128)} %pad_maximum_fusion.9), channel_id=1, source_target_pairs={{0,1},{1,2},{2,3},{3,4},{4,5},{5,6},{6,7},{8,9},{9,10},{10,11},{11... | collective-permute-start | bytes 1572872 | tf_op jit(solution)/shard_map/while/body/eval_jaxpr/ppermute | solution.py:21
  366.9 10.7 %collective-permute-start = (f32[2,1,4,128,128]{3,4,2,1,0:T(8,128)}, f32[2,1,4,128,128]{3,4,2,1,0:T(8,128)S(1)}, u32[]{:S(2)}, u32[]{:S(2)}) collective-permute-start(f32[2,1,4,128,128]{3,4,2,1,0:T(8,128)} %pad_maximum_fusion.9), channel_id=1, source_target_pairs={{0,1},{1,2},{2,3},{3,4},{4,5},{5,6},{6,7},{8,9},{9,10},{10,11},{11... | collective-permute-start | bytes 1572872 | tf_op jit(solution)/shard_map/while/body/eval_jaxpr/ppermute | solution.py:21
  385.2 10.7 %collective-permute-start = (f32[2,1,4,128,128]{3,4,2,1,0:T(8,128)}, f32[2,1,4,128,128]{3,4,2,1,0:T(8,128)S(1)}, u32[]{:S(2)}, u32[]{:S(2)}) collective-permute-start(f32[2,1,4,128,128]{3,4,2,1,0:T(8,128)} %pad_maximum_fusion.9), channel_id=1, source_target_pairs={{0,1},{1,2},{2,3},{3,4},{4,5},{5,6},{6,7},{8,9},{9,10},{10,11},{11... | collective-permute-start | bytes 1572872 | tf_op jit(solution)/shard_map/while/body/eval_jaxpr/ppermute | solution.py:21
  403.4 10.7 %collective-permute-start = (f32[2,1,4,128,128]{3,4,2,1,0:T(8,128)}, f32[2,1,4,128,128]{3,4,2,1,0:T(8,128)S(1)}, u32[]{:S(2)}, u32[]{:S(2)}) collective-permute-start(f32[2,1,4,128,128]{3,4,2,1,0:T(8,128)} %pad_maximum_fusion.9), channel_id=1, source_target_pairs={{0,1},{1,2},{2,3},{3,4},{4,5},{5,6},{6,7},{8,9},{9,10},{10,11},{11... | collective-permute-start | bytes 1572872 | tf_op jit(solution)/shard_map/while/body/eval_jaxpr/ppermute | solution.py:21
  421.7 10.7 %collective-permute-start = (f32[2,1,4,128,128]{3,4,2,1,0:T(8,128)}, f32[2,1,4,128,128]{3,4,2,1,0:T(8,128)S(1)}, u32[]{:S(2)}, u32[]{:S(2)}) collective-permute-start(f32[2,1,4,128,128]{3,4,2,1,0:T(8,128)} %pad_maximum_fusion.9), channel_id=1, source_target_pairs={{0,1},{1,2},{2,3},{3,4},{4,5},{5,6},{6,7},{8,9},{9,10},{10,11},{11... | collective-permute-start | bytes 1572872 | tf_op jit(solution)/shard_map/while/body/eval_jaxpr/ppermute | solution.py:21
  439.9 10.7 %collective-permute-start = (f32[2,1,4,128,128]{3,4,2,1,0:T(8,128)}, f32[2,1,4,128,128]{3,4,2,1,0:T(8,128)S(1)}, u32[]{:S(2)}, u32[]{:S(2)}) collective-permute-start(f32[2,1,4,128,128]{3,4,2,1,0:T(8,128)} %pad_maximum_fusion.9), channel_id=1, source_target_pairs={{0,1},{1,2},{2,3},{3,4},{4,5},{5,6},{6,7},{8,9},{9,10},{10,11},{11... | collective-permute-start | bytes 1572872 | tf_op jit(solution)/shard_map/while/body/eval_jaxpr/ppermute | solution.py:21
  458.2 10.7 %collective-permute-start = (f32[2,1,4,128,128]{3,4,2,1,0:T(8,128)}, f32[2,1,4,128,128]{3,4,2,1,0:T(8,128)S(1)}, u32[]{:S(2)}, u32[]{:S(2)}) collective-permute-start(f32[2,1,4,128,128]{3,4,2,1,0:T(8,128)} %pad_maximum_fusion.9), channel_id=1, source_target_pairs={{0,1},{1,2},{2,3},{3,4},{4,5},{5,6},{6,7},{8,9},{9,10},{10,11},{11... | collective-permute-start | bytes 1572872 | tf_op jit(solution)/shard_map/while/body/eval_jaxpr/ppermute | solution.py:21
  474.7 135.2 %copy-start = (f32[1,2,1,128,128]{4,3,2,1,0:T(8,128)S(1)}, f32[1,2,1,128,128]{4,3,2,1,0:T(8,128)}, u32[]{:S(2)}) copy-start(f32[1,2,1,128,128]{4,3,2,1,0:T(8,128)} %reduce-scatter.2.cloned.1.call-done) | copy-start | bytes 393220
  481.3 8.9 %collective-permute-start.1 = (f32[2,1,4,128,128]{3,4,2,1,0:T(8,128)}, f32[2,1,4,128,128]{3,4,2,1,0:T(8,128)S(1)}, u32[]{:S(2)}, u32[]{:S(2)}) collective-permute-start(f32[2,1,4,128,128]{3,4,2,1,0:T(8,128)} %pad_maximum_fusion.10), channel_id=1, source_target_pairs={{1,0},{2,1},{3,2},{4,3},{5,4},{6,5},{7,6},{9,8},{10,9},{11,10},{12... | collective-permute-start | bytes 1572872 | tf_op jit(solution)/shard_map/while/body/eval_jaxpr/ppermute | solution.py:21
  496.6 10.7 %collective-permute-start.1 = (f32[2,1,4,128,128]{3,4,2,1,0:T(8,128)}, f32[2,1,4,128,128]{3,4,2,1,0:T(8,128)S(1)}, u32[]{:S(2)}, u32[]{:S(2)}) collective-permute-start(f32[2,1,4,128,128]{3,4,2,1,0:T(8,128)} %pad_maximum_fusion.10), channel_id=1, source_target_pairs={{1,0},{2,1},{3,2},{4,3},{5,4},{6,5},{7,6},{9,8},{10,9},{11,10},{12... | collective-permute-start | bytes 1572872 | tf_op jit(solution)/shard_map/while/body/eval_jaxpr/ppermute | solution.py:21
  513.7 10.7 %collective-permute-start.1 = (f32[2,1,4,128,128]{3,4,2,1,0:T(8,128)}, f32[2,1,4,128,128]{3,4,2,1,0:T(8,128)S(1)}, u32[]{:S(2)}, u32[]{:S(2)}) collective-permute-start(f32[2,1,4,128,128]{3,4,2,1,0:T(8,128)} %pad_maximum_fusion.10), channel_id=1, source_target_pairs={{1,0},{2,1},{3,2},{4,3},{5,4},{6,5},{7,6},{9,8},{10,9},{11,10},{12... | collective-permute-start | bytes 1572872 | tf_op jit(solution)/shard_map/while/body/eval_jaxpr/ppermute | solution.py:21
  530.8 10.7 %collective-permute-start.1 = (f32[2,1,4,128,128]{3,4,2,1,0:T(8,128)}, f32[2,1,4,128,128]{3,4,2,1,0:T(8,128)S(1)}, u32[]{:S(2)}, u32[]{:S(2)}) collective-permute-start(f32[2,1,4,128,128]{3,4,2,1,0:T(8,128)} %pad_maximum_fusion.10), channel_id=1, source_target_pairs={{1,0},{2,1},{3,2},{4,3},{5,4},{6,5},{7,6},{9,8},{10,9},{11,10},{12... | collective-permute-start | bytes 1572872 | tf_op jit(solution)/shard_map/while/body/eval_jaxpr/ppermute | solution.py:21
  547.9 10.7 %collective-permute-start.1 = (f32[2,1,4,128,128]{3,4,2,1,0:T(8,128)}, f32[2,1,4,128,128]{3,4,2,1,0:T(8,128)S(1)}, u32[]{:S(2)}, u32[]{:S(2)}) collective-permute-start(f32[2,1,4,128,128]{3,4,2,1,0:T(8,128)} %pad_maximum_fusion.10), channel_id=1, source_target_pairs={{1,0},{2,1},{3,2},{4,3},{5,4},{6,5},{7,6},{9,8},{10,9},{11,10},{12... | collective-permute-start | bytes 1572872 | tf_op jit(solution)/shard_map/while/body/eval_jaxpr/ppermute | solution.py:21
  565.0 10.7 %collective-permute-start.1 = (f32[2,1,4,128,128]{3,4,2,1,0:T(8,128)}, f32[2,1,4,128,128]{3,4,2,1,0:T(8,128)S(1)}, u32[]{:S(2)}, u32[]{:S(2)}) collective-permute-start(f32[2,1,4,128,128]{3,4,2,1,0:T(8,128)} %pad_maximum_fusion.10), channel_id=1, source_target_pairs={{1,0},{2,1},{3,2},{4,3},{5,4},{6,5},{7,6},{9,8},{10,9},{11,10},{12... | collective-permute-start | bytes 1572872 | tf_op jit(solution)/shard_map/while/body/eval_jaxpr/ppermute | solution.py:21
  582.1 10.7 %collective-permute-start.1 = (f32[2,1,4,128,128]{3,4,2,1,0:T(8,128)}, f32[2,1,4,128,128]{3,4,2,1,0:T(8,128)S(1)}, u32[]{:S(2)}, u32[]{:S(2)}) collective-permute-start(f32[2,1,4,128,128]{3,4,2,1,0:T(8,128)} %pad_maximum_fusion.10), channel_id=1, source_target_pairs={{1,0},{2,1},{3,2},{4,3},{5,4},{6,5},{7,6},{9,8},{10,9},{11,10},{12... | collective-permute-start | bytes 1572872 | tf_op jit(solution)/shard_map/while/body/eval_jaxpr/ppermute | solution.py:21
  599.1 10.7 %collective-permute-start.1 = (f32[2,1,4,128,128]{3,4,2,1,0:T(8,128)}, f32[2,1,4,128,128]{3,4,2,1,0:T(8,128)S(1)}, u32[]{:S(2)}, u32[]{:S(2)}) collective-permute-start(f32[2,1,4,128,128]{3,4,2,1,0:T(8,128)} %pad_maximum_fusion.10), channel_id=1, source_target_pairs={{1,0},{2,1},{3,2},{4,3},{5,4},{6,5},{7,6},{9,8},{10,9},{11,10},{12... | collective-permute-start | bytes 1572872 | tf_op jit(solution)/shard_map/while/body/eval_jaxpr/ppermute | solution.py:21
Sparse Core Ops, SparseCore 0:
  97.2 224.3 reduce-scatter.1
  611.0 80.9 all-gather.1
where the time goes:
time: 875 us; the launch traced here: 864 us
  waiting for transfers between devices  429 us (49%)
  local copies, waits for them, and re-layouts  178 us (20%)
  matrix products  78.1 us (9%)
  other arithmetic  73.3 us (8%)
  loops' own time  45.3 us (5%)
  starting transfers between devices  43.2 us (5%)
  between operations  17 us (2%)
    reduce_scatter x1, waiting for transfers between devices, local(): lax.psum_scatter(jax.vmap(extract)(row_offsets, col_offsets), 'tile', sca...  224 us
    ppermute x16, waiting for transfers between devices, shifted(): lax.ppermute(value, axis, [(source, source + steps) for source in range(f...  124 us
    gather x96, local copies, waits for them, and re-layouts  84.2 us
    all_gather x1, waiting for transfers between devices, local(): part_rows = lax.all_gather(window_grads, 'tile', axis=0, tiled=True)  81.1 us
    dynamic_update_slice x32, local copies, waits for them, and re-layouts, add_one(): return lax.dynamic_update_slice(running, current + addend, where_at)  50.5 us
    ppermute x16, starting transfers between devices, shifted(): lax.ppermute(value, axis, [(source, source + steps) for source in range(f...  43.1 us
    another operation x1, loops' own time, local(): deposit_sum = lax.fori_loop(0, part_rows.shape[0], add_one, empty_tile)  43 us
    add x32, other arithmetic, add_one(): return lax.dynamic_update_slice(running, current + addend, where_at)  32.5 us
  transfers between devices with their start and end apart: 18, of which 18 were waited for; matrix products, arithmetic and copies ran while one was open for 0% of the time, Pallas kernels for 0%

commit v1 on v0

v1 whole, which is shorter than its diff:
```python
import functools
import math

import numpy as np
import jax
import jax.numpy as jnp
from jax import lax
from jax.experimental import pallas as pl
from jax.experimental.pallas import tpu as pltpu
from jax.sharding import PartitionSpec as P

W = 128
MODES = 4
TS = 384
GY = 4
POS = 32
NZ = 8
NY = 4
DEPTH = 8
CHUNKS = TS // W + 2
PADDED = TS + 2 * W

count_scale = 0.0078125
loss_scale = 0.03125
fresnel_strength = 40.0

VMEM = pl.BlockSpec(memory_space=pltpu.VMEM)
SMEM = pl.BlockSpec(memory_space=pltpu.SMEM)
ANY = pl.BlockSpec(memory_space=pl.ANY)
MESH = pl.DeviceIdType.MESH


def make_tables():
    index = np.arange(W)
    angle = 2.0 * np.pi * ((index[:, None] * index[None, :]) % W) / W
    dft = np.exp(-1j * angle) / math.sqrt(W)
    signed = ((index + W // 2) % W - W // 2) / W
    chirp = np.exp(-1j * fresnel_strength * signed**2)
    step = np.conj(dft) @ (chirp[:, None] * dft)
    tables = []
    for g in (step, dft):
        right = np.block([[g.real, g.imag], [-g.imag, g.real]])
        for table in (right, right.T):
            table = table.astype(np.float32)
            high = table.astype(jnp.bfloat16)
            low = (table - high.astype(np.float32)).astype(jnp.bfloat16)
            tables.append(np.stack([high, low]))
    return np.stack(tables)


def tile_corner(slots, me):
    def look(i, place):
        return jnp.where(slots[i] == me, i, place)

    place = lax.fori_loop(0, POS, look, jnp.int32(0))
    row = place // GY
    return row * TS, (place - row * GY) * TS


def overlap(rows, cols, p, top, left):
    dr = rows[p] - top
    dc = cols[p] - left
    return dr, dc, (dr > -W) & (dr < TS) & (dc > -W) & (dc < TS)


def extract_kernel(rows, cols, slots, phase, absorb, out, padded):
    me = lax.axis_index("tile")
    top, left = tile_corner(slots, me)
    padded[...] = jnp.zeros_like(padded)
    for m, source in enumerate((phase, absorb)):
        for c in range(CHUNKS - 2):
            padded[m, c + 1, W : W + TS, :] = source[0, 0, :, c * W : (c + 1) * W]
    lane = lax.broadcasted_iota(jnp.int32, (W, W), 1)

    def one(p, carry):
        dr, dc, touches = overlap(rows, cols, p, top, left)

        @pl.when(touches)
        def _():
            start = dr + W
            chunk = (dc + W) // W
            shift = dc + W - chunk * W
            turn = jnp.where(shift == 0, 0, W - shift)
            for m in range(2):
                first = padded[m, chunk, pl.ds(start, W), :]
                second = padded[m, chunk + 1, pl.ds(start, W), :]
                out[p, m] = jnp.where(
                    lane < W - shift, pltpu.roll(first, turn, 1), pltpu.roll(second, turn, 1)
                )

        @pl.when(jnp.logical_not(touches))
        def _():
            out[p] = jnp.zeros((2, W, W), jnp.float32)

        return carry

    lax.fori_loop(0, POS, one, 0)


def deposit_kernel(rows, cols, slots, grads, phase_out, absorb_out, acc, held, sems):
    me = lax.axis_index("tile")
    top, left = tile_corner(slots, me)

    def fetch(p):
        return pltpu.make_async_copy(grads.at[p], held.at[p], sems.at[p])

    def begin(p, carry):
        dr, dc, touches = overlap(rows, cols, p, top, left)

        @pl.when(touches)
        def _():
            fetch(p).start()

        return carry

    lax.fori_loop(0, POS, begin, 0)
    acc[...] = jnp.zeros_like(acc)
    lane = lax.broadcasted_iota(jnp.int32, (W, W), 1)

    def one(p, carry):
        dr, dc, touches = overlap(rows, cols, p, top, left)

        @pl.when(touches)
        def _():
            fetch(p).wait()
            start = dr + W
            chunk = (dc + W) // W
            shift = dc + W - chunk * W
            for m in range(2):
                turned = pltpu.roll(held[p, m], shift, 1)
                acc[m, chunk, pl.ds(start, W), :] += jnp.where(lane >= shift, turned, 0.0)
                acc[m, chunk + 1, pl.ds(start, W), :] += jnp.where(lane < shift, turned, 0.0)

        return carry

    lax.fori_loop(0, POS, one, 0)
    for m, target in enumerate((phase_out, absorb_out)):
        for c in range(CHUNKS - 2):
            target[0, 0, :, c * W : (c + 1) * W] = acc[m, c + 1, W : W + TS, :]


def tile_place():
    me = lax.axis_index("tile")
    z = me // NY
    return z, me - z * NY


def turned(value, step, count):
    return lax.rem(value + step + count, count)


def greet(partners):
    barrier = pltpu.get_barrier_semaphore()
    for partner in partners:
        pl.semaphore_signal(barrier, inc=1, device_id=partner, device_id_type=MESH)
    pl.semaphore_wait(barrier, len(partners))


def tile_partners(z, y):
    return [
        {"tile": turned(z, 1, NZ) * NY + y},
        {"tile": turned(z, -1, NZ) * NY + y},
        {"tile": z * NY + turned(y, 1, NY)},
        {"tile": z * NY + turned(y, -1, NY)},
        {"tile": z * NY + turned(y, 2, NY)},
    ]


class Sender:
    def __init__(self, send_sems, recv_sems):
        self.send_sems, self.recv_sems = send_sems, recv_sems
        self.used = 0
        self.started = []

    def copy(self, source, target, device):
        n = self.used
        self.used += 1
        copy = pltpu.make_async_remote_copy(
            src_ref=source,
            dst_ref=target,
            send_sem=self.send_sems.at[n],
            recv_sem=self.recv_sems.at[n],
            device_id=device,
            device_id_type=MESH,
        )
        copy.start()
        self.started.append(copy)
        return copy

    def finish(self):
        for copy in self.started:
            copy.wait_send()


def ring_streams(count, streams):
    plan = []
    for stream in range(streams):
        first = stream < streams // 2
        plan.append((stream, 1, count // 2 if first else count // 2 - 1))
        plan.append((stream, -1, count // 2 - 1 if first else count // 2))
    return plan


SCATTER_COPIES = 28 + 3 + 24 + 14
HALF = W // 2


def scatter_kernel(ext, out, a_recv, a_side, b_recv, b_recv2, send_sems, recv_sems):
    z, y = tile_place()
    greet(tile_partners(z, y))
    send = Sender(send_sems, recv_sems)

    def z_device(way):
        return {"tile": turned(z, way, NZ) * NY + y}

    def y_device(step):
        return {"tile": z * NY + turned(y, step, NY)}

    a_last = {}
    a_slot = [0]

    def a_step(s):
        for stream, way, length in ring_streams(NZ, NY):
            if s >= length:
                continue
            dest = turned(z, way * (length - s), NZ) * NY + stream
            if s > 0:
                copy, slot = a_last[stream, way]
                copy.wait_recv()
                a_recv[slot] += ext[dest, 0]
                source = a_recv.at[slot]
            else:
                source = ext.at[dest, 0]
            slot = a_slot[0]
            a_slot[0] += 1
            copy = send.copy(source, a_recv.at[slot], z_device(way))
            a_last[stream, way] = (copy, slot)

    b_last = {}
    b_slot = [0]

    def b_step(s):
        for stream in range(NZ):
            for way in (1, -1):
                length = 2 if (stream % 2 == 0) == (way == 1) else 1
                if s >= length:
                    continue
                dest = stream * NY + turned(y, way * (length - s), NY)
                if s > 0:
                    copy, slot = b_last[stream, way]
                    copy.wait_recv()
                    b_recv[slot] += ext[dest, 1]
                    source = b_recv.at[slot]
                else:
                    source = ext.at[dest, 1]
                slot = b_slot[0]
                b_slot[0] += 1
                copy = send.copy(source, b_recv.at[slot], y_device(way))
                b_last[stream, way] = (copy, slot)

    a_step(0)
    b_step(0)
    a_step(1)
    b_step(1)
    a_step(2)
    for stream in range(NZ):
        mine = stream * NY + y
        total = ext[mine, 1]
        for way in (1, -1):
            copy, slot = b_last[stream, way]
            copy.wait_recv()
            total = total + b_recv[slot]
        b_recv2[stream] = total
    c_last = {}
    c_slot = [0]

    def c_step(s):
        for stream, way, length in ring_streams(NZ, 2):
            if s >= length:
                continue
            dest = turned(z, way * (length - s), NZ)
            part = pl.ds(stream * HALF, HALF)
            if s > 0:
                copy, slot = c_last[stream, way]
                copy.wait_recv()
                b_recv2[NZ + slot, :HALF] += b_recv2[dest, part]
                source = b_recv2.at[NZ + slot, pl.ds(0, HALF)]
            else:
                source = b_recv2.at[dest, part]
            slot = c_slot[0]
            c_slot[0] += 1
            copy = send.copy(source, b_recv2.at[NZ + slot, pl.ds(0, HALF)], z_device(way))
            c_last[stream, way] = (copy, slot)

    c_step(0)
    a_step(3)
    c_step(1)
    a_copies = []
    for stream in range(NY):
        mine = z * NY + stream
        total = ext[mine, 0]
        for way in (1, -1):
            copy, slot = a_last[stream, way]
            copy.wait_recv()
            total = total + a_recv[slot]
        a_side[stream] = total
    for step in (1, 2, 3):
        a_copies.append(
            send.copy(a_side.at[turned(y, step, NY)], a_side.at[NY + step], y_device(step))
        )
    c_step(2)
    c_step(3)
    total = a_side[y]
    for step, copy in zip((1, 2, 3), a_copies):
        copy.wait_recv()
        total = total + a_side[NY + step]
    out[0] = total
    for stream in range(2):
        part = pl.ds(stream * HALF, HALF)
        total = b_recv2[z, part]
        for way in (1, -1):
            copy, slot = c_last[stream, way]
            copy.wait_recv()
            total = total + b_recv2[NZ + slot, :HALF]
        out[1, part] = total
    send.finish()


GATHER_COPIES = 14 + 24 + 3 + 28


def gather_kernel(own, out, send_sems, recv_sems):
    z, y = tile_place()
    greet(tile_partners(z, y))
    send = Sender(send_sems, recv_sems)
    me = z * NY + y

    def z_device(way):
        return {"tile": turned(z, way, NZ) * NY + y}

    def y_device(step):
        return {"tile": z * NY + turned(y, step, NY)}

    out[me] = own[...]

    b_copies = {0: None}
    for step in (1, 3, 2):
        b_copies[step] = send.copy(out.at[me, 1], out.at[me, 1], y_device(step))

    c_last = {}

    def c_step(s):
        for stream, way, length in ring_streams(NZ, 2):
            chunk = turned(z, -way * s, NZ) * NY + y
            part = pl.ds(stream * HALF, HALF)
            if s > 0:
                c_last[stream, way].wait_recv()
            if s >= length:
                continue
            c_last[stream, way] = send.copy(
                out.at[chunk, 0, part], out.at[chunk, 0, part], z_device(way)
            )

    a_last = {}

    def a_step(s):
        for stream, way, length in ring_streams(NZ, NY):
            if s >= length:
                continue
            column = turned(y, -stream, NY)
            chunk = turned(z, -way * s, NZ) * NY + column
            if s > 0:
                a_last[stream, way].wait_recv()
            elif way == 1 and b_copies[stream] is not None:
                b_copies[stream].wait_recv()
            a_last[stream, way] = send.copy(out.at[chunk, 1], out.at[chunk, 1], z_device(way))

    b_last = {}

    def b_first(offset):
        for way in (1, -1):
            chunk = turned(z, offset, NZ) * NY + y
            b_last[offset % NZ, way] = send.copy(out.at[chunk, 0], out.at[chunk, 0], y_device(way))

    def b_second(offset):
        offset = offset % NZ
        way = 1 if offset % 2 == 0 else -1
        b_last[offset, way].wait_recv()
        chunk = turned(z, offset, NZ) * NY + turned(y, -way, NY)
        b_last[offset, 2] = send.copy(out.at[chunk, 0], out.at[chunk, 0], y_device(way))

    c_step(0)
    b_first(0)
    a_step(0)
    for s in range(1, NZ // 2):
        c_step(s)
        b_first(-s)
        b_first(s)
        a_step(s)
        b_second(s - 1)
        if s > 1:
            b_second(1 - s)
    c_last[0, 1].wait_recv()
    c_last[1, -1].wait_recv()
    b_first(NZ // 2)
    b_second(NZ // 2 - 1)
    b_second(1 - NZ // 2)
    b_second(NZ // 2)
    for offset in range(NZ):
        forwarded = 1 if offset % 2 == 0 else -1
        b_last[offset, -forwarded].wait_recv()
        b_last[offset, 2].wait_recv()
    for stream, way, length in ring_streams(NZ, NY):
        a_last[stream, way].wait_recv()
    send.finish()


def split(value):
    high = value.astype(jnp.bfloat16)
    low = (value - high.astype(jnp.float32)).astype(jnp.bfloat16)
    return high, low


def mxu(a, b):
    return jnp.dot(a, b, preferred_element_type=jnp.float32)


def transform(real, imag, tables, right, left):
    high, low = split(jnp.concatenate([real, imag], 1))
    half = mxu(high, tables[right, 0]) + (mxu(low, tables[right, 0]) + mxu(high, tables[right, 1]))
    high, low = split(jnp.concatenate([half[:, :W], half[:, W:]], 0))
    done = mxu(tables[left, 0], jnp.concatenate([high, low], 1))
    done = done[:, :W] + (done[:, W:] + mxu(tables[left, 1], high))
    return done[:W], done[W:]


STEP, STEP_BACK, DFT, DFT_BACK = (0, 1), (1, 0), (2, 3), (3, 2)


def chain_kernel(
    windows, probe, counts, tables, out,
    trans, waves, shares, grads, got,
    t_send, t_recv, i_send, i_recv, g_send, g_recv,
):
    d = lax.axis_index("depth")
    x = d // 2
    core = d - x * 2
    greet([{"depth": turned(d, k, DEPTH)} for k in range(1, DEPTH)])

    damping = jnp.exp(-windows[1])
    trans[d, 0] = damping * jnp.cos(windows[0])
    trans[d, 1] = damping * jnp.sin(windows[0])

    def trans_copy(k):
        return pltpu.make_async_remote_copy(
            src_ref=trans.at[d],
            dst_ref=trans.at[d],
            send_sem=t_send.at[k],
            recv_sem=t_recv.at[d],
            device_id={"depth": turned(x, k, MODES) * 2},
            device_id_type=MESH,
        )

    for k in (1, 3, 2):
        trans_copy(k).start()

    @pl.when(core == 1)
    def _():
        trans_copy(0).start()

    def share_copy(k):
        return pltpu.make_async_remote_copy(
            src_ref=shares.at[0],
            dst_ref=shares.at[k],
            send_sem=i_send.at[k],
            recv_sem=i_recv.at[k],
            device_id={"depth": turned(x, k, MODES) * 2},
            device_id_type=MESH,
        )

    def grad_copy(j):
        return pltpu.make_async_remote_copy(
            src_ref=grads.at[j],
            dst_ref=got.at[x],
            send_sem=g_send.at[j],
            recv_sem=g_recv.at[x],
            device_id={"depth": j},
            device_id_type=MESH,
        )

    @pl.when(core == 0)
    def _():
        real, imag = probe[0, x], probe[1, x]
        for j in range(DEPTH):
            waves[j, 0] = real
            waves[j, 1] = imag

            @pl.when(d != j)
            def _():
                pltpu.make_async_remote_copy(
                    src_ref=trans.at[j],
                    dst_ref=trans.at[j],
                    send_sem=t_send.at[0],
                    recv_sem=t_recv.at[j],
                    device_id={"depth": turned(d, 1, DEPTH)},
                    device_id_type=MESH,
                ).wait_recv()

            tr, ti = trans[j, 0], trans[j, 1]
            table = STEP if j < DEPTH - 1 else DFT
            real, imag = transform(
                tr * real - ti * imag, tr * imag + ti * real, tables, *table
            )
        shares[0] = real * real + imag * imag
        for k in (1, 3, 2):
            share_copy(k).start()
        residual = shares[0] - count_scale * counts[0].astype(jnp.float32)
        for k in (1, 3, 2):
            share_copy(k).wait_recv()
            residual = residual + shares[k]
        residual = (4.0 * loss_scale) * residual
        real, imag = residual * real, residual * imag
        for j in reversed(range(DEPTH)):
            table = STEP_BACK if j < DEPTH - 1 else DFT_BACK
            real, imag = transform(real, imag, tables, *table)
            tr, ti = trans[j, 0], trans[j, 1]
            real, imag = tr * real + ti * imag, tr * imag - ti * real
            wr, wi = waves[j, 0], waves[j, 1]
            grads[j, 0] = wr * imag - wi * real
            grads[j, 1] = -(wr * real + wi * imag)

            @pl.when(d != j)
            def _():
                grad_copy(j).start()

            @pl.when(d == j)
            def _():
                got[x] = grads[j]

        for k in (1, 3, 2):
            share_copy(k).wait_send()
        for j in range(DEPTH):

            @pl.when(d != j)
            def _():
                grad_copy(j).wait_send()

    for k in (1, 3, 2):
        trans_copy(k).wait_send()

    @pl.when(core == 1)
    def _():
        trans_copy(0).wait_send()

    for k in range(MODES):

        @pl.when(d != 2 * k)
        def _():
            pltpu.make_async_remote_copy(
                src_ref=got.at[k],
                dst_ref=got.at[k],
                send_sem=g_send.at[0],
                recv_sem=g_recv.at[k],
                device_id={"depth": turned(d, 1, DEPTH)},
                device_id_type=MESH,
            ).wait_recv()

    out[...] = (got[0] + got[1]) + (got[2] + got[3])


def local(phase, absorb, probe, row_offsets, col_offsets, tile_slot, counts):
    f32 = jnp.float32
    mib = 1 << 20
    dma = pltpu.SemaphoreType.DMA
    parts = pl.pallas_call(
        extract_kernel,
        out_shape=jax.ShapeDtypeStruct((POS, 2, W, W), f32),
        in_specs=[SMEM, SMEM, SMEM, VMEM, VMEM],
        out_specs=VMEM,
        scratch_shapes=[pltpu.VMEM((2, CHUNKS, PADDED, W), f32)],
        compiler_params=pltpu.CompilerParams(vmem_limit_bytes=24 * mib),
        name="extract",
    )(row_offsets, col_offsets, tile_slot, phase, absorb)
    windows = pl.pallas_call(
        scatter_kernel,
        out_shape=jax.ShapeDtypeStruct((2, W, W), f32),
        in_specs=[VMEM],
        out_specs=VMEM,
        scratch_shapes=[
            pltpu.VMEM((28, W, W), f32),
            pltpu.VMEM((2 * NY, W, W), f32),
            pltpu.VMEM((24, W, W), f32),
            pltpu.VMEM((NZ + 14, W, W), f32),
            dma((SCATTER_COPIES,)),
            dma((SCATTER_COPIES,)),
        ],
        compiler_params=pltpu.CompilerParams(
            collective_id=0, has_side_effects=True, vmem_limit_bytes=24 * mib
        ),
        name="scatter",
    )(parts)
    grads = pl.pallas_call(
        chain_kernel,
        out_shape=jax.ShapeDtypeStruct((2, W, W), f32),
        in_specs=[VMEM] * 4,
        out_specs=VMEM,
        scratch_shapes=[
            pltpu.VMEM((DEPTH, 2, W, W), f32),
            pltpu.VMEM((DEPTH, 2, W, W), f32),
            pltpu.VMEM((MODES, W, W), f32),
            pltpu.VMEM((DEPTH, 2, W, W), f32),
            pltpu.VMEM((MODES, 2, W, W), f32),
            dma((MODES,)),
            dma((DEPTH,)),
            dma((MODES,)),
            dma((MODES,)),
            dma((DEPTH,)),
            dma((MODES,)),
        ],
        compiler_params=pltpu.CompilerParams(
            collective_id=1, has_side_effects=True, vmem_limit_bytes=24 * mib
        ),
        name="chain",
    )(windows, probe, counts, jnp.asarray(make_tables()))
    gathered = pl.pallas_call(
        gather_kernel,
        out_shape=jax.ShapeDtypeStruct((POS, 2, W, W), f32),
        in_specs=[VMEM],
        out_specs=VMEM,
        scratch_shapes=[dma((GATHER_COPIES,)), dma((GATHER_COPIES,))],
        compiler_params=pltpu.CompilerParams(
            collective_id=2, has_side_effects=True, vmem_limit_bytes=24 * mib
        ),
        name="gather",
    )(grads)
    return pl.pallas_call(
        deposit_kernel,
        out_shape=(jax.ShapeDtypeStruct((1, 1, TS, TS), f32),) * 2,
        in_specs=[SMEM, SMEM, SMEM, ANY],
        out_specs=(VMEM, VMEM),
        scratch_shapes=[
            pltpu.VMEM((2, CHUNKS, PADDED, W), f32),
            pltpu.VMEM((POS, 2, W, W), f32),
            dma((POS,)),
        ],
        compiler_params=pltpu.CompilerParams(vmem_limit_bytes=24 * mib),
        name="deposit",
    )(row_offsets, col_offsets, tile_slot, gathered)


def solution(mesh):
    in_specs = (
        P("depth", "tile", None, None),
        P("depth", "tile", None, None),
        P(),
        P(),
        P(),
        P(),
        P("tile", None, None),
    )
    out_specs = (P("depth", "tile", None, None), P("depth", "tile", None, None))
    return jax.shard_map(local, mesh=mesh, in_specs=in_specs, out_specs=out_specs, check_vma=False)
```

time: 875 us -> 119 us (0.14); the launches traced: 864 us -> 119 us
  waiting for transfers between devices: 429 us -> 0 us
  local copies, waits for them, and re-layouts: 178 us -> 4.21 us
  Pallas kernels: 0 us -> 114 us
  matrix products: 78.1 us -> 0 us
  other arithmetic: 73.3 us -> 0 us
  loops' own time: 45.3 us -> 0 us
  starting transfers between devices: 43.2 us -> 0 us
  between operations: 17 us -> 0.75 us
    reduce_scatter x1 -> x0, waiting for transfers between devices: 224 us -> none  [local(): lax.psum_scatter(jax.vmap(extract)(row_offsets, col_offsets), 'tile', sca...]
    ppermute x16 -> x0, waiting for transfers between devices: 124 us -> none  [shifted(): lax.ppermute(value, axis, [(source, source + steps) for source in range(f...]
    pallas_call x0 -> x5, Pallas kernels: none -> 114 us  [the longest x1 40.5 us: local(): pl.pallas_call(scatter_kernel, out_shape=jax.ShapeDtypeStruct((2, W, W),...]
    gather x96 -> x0, local copies, waits for them, and re-layouts: 84.2 us -> none
    all_gather x1 -> x0, waiting for transfers between devices: 81.1 us -> none  [local(): part_rows = lax.all_gather(window_grads, 'tile', axis=0, tiled=True)]
    dot_general x102 -> x0, matrix products: 78.1 us -> none  [the longest x34 27.8 us: transform(): jnp.einsum('ij,...jk->...ik', sin_t, half_done, precision=lax.Precision.H...]
    dynamic_update_slice x32 -> x0, local copies, waits for them, and re-layouts: 50.5 us -> none  [add_one(): return lax.dynamic_update_slice(running, current + addend, where_at)]
    another operation x4 -> x0, loops' own time: 45.3 us -> none  [the longest x1 43 us: local(): deposit_sum = lax.fori_loop(0, part_rows.shape[0], add_one, empty_tile)]
  transfers between devices with their start and end apart: 18 -> 0, of which waited for: 18 -> 0; matrix products, arithmetic and copies ran while one was open for 0% -> 0% of each run, Pallas kernels for 0% -> 0%
where the time goes in v1:
time: 119 us
  Pallas kernels  114 us (96%)
  local copies, waits for them, and re-layouts  4.21 us (4%)
    pallas_call x1, Pallas kernels, local(): pl.pallas_call(scatter_kernel, out_shape=jax.ShapeDtypeStruct((2, W, W),...  40.5 us
    pallas_call x1, Pallas kernels, local(): pl.pallas_call(gather_kernel, out_shape=jax.ShapeDtypeStruct((POS, 2, W,...  36.9 us
    pallas_call x1, Pallas kernels, local(): pl.pallas_call(chain_kernel, out_shape=jax.ShapeDtypeStruct((2, W, W), f3...  29.8 us
    unnamed x22, local copies, waits for them, and re-layouts  4.21 us
    pallas_call x1, Pallas kernels, local(): pl.pallas_call(deposit_kernel, out_shape=(jax.ShapeDtypeStruct((1, 1, TS,...  4.15 us

profile of v1, /device:TPU:2, one launch (start us, length us, event | category | flops | bytes accessed | tf_op | source)
XLA Modules:
  0.0 118.5 jit_solution(1037899113227923672)
XLA Ops:
  0.6 0.0 copy-start
  0.6 0.0 copy-start.1
  0.7 1.1 copy-done.1
  1.8 0.0 copy-start.2
  1.8 1.1 copy-done.2
  2.9 0.0 copy-start.5
  2.9 0.7 copy-done.5
  3.5 0.0 copy-start.7
  3.5 0.7 copy-done.7
  4.2 0.7 copy-done.9
  4.8 2.2 %extract.1.ext = f32[32,2,128,128]{3,2,1,0:T(8,128)S(1)} custom-call(s32[32]{0:T(128)S(1)} %copy-done.5, s32[32]{0:T(128)S(1)} %copy-done.7, s32[32]{0:T(128)S(1)} %copy-done.9, f32[1,1,384,384]{3,2,1,0:T(8,128)S(1)} %copy-done.1, f32[1,1,384,384]{3,2,1,0:T(8,128)S(1)} %copy-done.2), custom_call_target="tpu_custom_call" | custom-call | tf_op jit(solution)/shard_map/extract/pallas_call | solution.py:575
  7.1 0.0 copy-start.6
  7.1 0.0 copy-start.8
  7.1 0.0 copy-start.10
  7.1 40.5 %scatter.1.windows = f32[2,128,128]{2,1,0:T(8,128)S(1)} custom-call(f32[32,2,128,128]{3,2,1,0:T(8,128)S(1)} %extract.1.ext), custom_call_target="tpu_custom_call" | custom-call | tf_op jit(solution)/shard_map/scatter/pallas_call | solution.py:584
  47.6 0.0 copy-done
  47.6 0.0 copy-done.3
  47.6 0.0 copy-done.4
  47.6 29.8 %chain.1.own = f32[2,128,128]{2,1,0:T(8,128)S(1)} custom-call(f32[2,128,128]{2,1,0:T(8,128)S(1)} %scatter.1.windows, f32[2,4,128,128]{3,2,1,0:T(8,128)S(1)} %copy-done.3, s32[1,128,128]{2,1,0:T(8,128)S(1)} %copy-done.4, bf16[4,2,256,256]{3,2,1,0:T(8,128)(2,1)S(1)} %copy-done), custom_call_target="tpu_custom_call" | custom-call | tf_op jit(solution)/shard_map/chain/pallas_call | solution.py:602
  77.4 36.9 %gather.1.grads = f32[32,2,128,128]{3,2,1,0:T(8,128)S(1)} custom-call(f32[2,128,128]{2,1,0:T(8,128)S(1)} %chain.1.own), custom_call_target="tpu_custom_call" | custom-call | tf_op jit(solution)/shard_map/gather/pallas_call | solution.py:625
  114.3 0.0 copy-done.6
  114.4 0.0 copy-done.8
  114.4 0.0 copy-done.10
  114.4 4.2 %deposit.1 = (f32[1,1,384,384]{3,2,1,0:T(8,128)}, f32[1,1,384,384]{3,2,1,0:T(8,128)}) custom-call(s32[32]{0:T(128)S(1)} %copy-done.6, s32[32]{0:T(128)S(1)} %copy-done.8, s32[32]{0:T(128)S(1)} %copy-done.10, f32[32,2,128,128]{3,2,1,0:T(8,128)S(1)} %gather.1.grads), custom_call_target="tpu_custom_call" | custom-call | tf_op jit(solution)/shard_map/deposit/pallas_call | solution.py:636
  (3 shorter events, 0.0 us)
Async XLA Ops:
  0.6 47.0 %copy-start = (bf16[4,2,256,256]{3,2,1,0:T(8,128)(2,1)S(1)}, bf16[4,2,256,256]{3,2,1,0:T(8,128)(2,1)}, u32[]{:S(2)}) copy-start(bf16[4,2,256,256]{3,2,1,0:T(8,128)(2,1)} %constant.2.clone.tables) | copy-start | bytes 3145732
  0.6 1.2 copy-start.1
  1.8 1.1 copy-start.2
  2.9 0.7 copy-start.5
  3.5 0.7 copy-start.7
  4.2 0.7 copy-start.9
  4.8 42.8 %copy-start.3 = (f32[2,4,128,128]{3,2,1,0:T(8,128)S(1)}, f32[2,4,128,128]{3,2,1,0:T(8,128)}, u32[]{:S(2)}) copy-start(f32[2,4,128,128]{3,2,1,0:T(8,128)} %probe.1) | copy-start | bytes 1572868
  4.8 42.8 %copy-start.4 = (s32[1,128,128]{2,1,0:T(8,128)S(1)}, s32[1,128,128]{2,1,0:T(8,128)}, u32[]{:S(2)}) copy-start(s32[1,128,128]{2,1,0:T(8,128)} %counts.1) | copy-start | bytes 196612
  7.1 107.3 %copy-start.6 = (s32[32]{0:T(128)S(1)}, s32[32]{0:T(128)}, u32[]{:S(2)}) copy-start(s32[32]{0:T(128)} %rows.3) | copy-start | bytes 388
  7.1 107.3 %copy-start.8 = (s32[32]{0:T(128)S(1)}, s32[32]{0:T(128)}, u32[]{:S(2)}) copy-start(s32[32]{0:T(128)} %cols.3) | copy-start | bytes 388
  7.1 107.3 %copy-start.10 = (s32[32]{0:T(128)S(1)}, s32[32]{0:T(128)}, u32[]{:S(2)}) copy-start(s32[32]{0:T(128)} %slots.3) | copy-start | bytes 388

commit v2 on v0

v2 whole, which is shorter than its diff:
```python
import functools
import math

import numpy as np
import jax
import jax.numpy as jnp
from jax import lax
from jax.experimental import pallas as pl
from jax.experimental.pallas import tpu as pltpu
from jax.sharding import PartitionSpec as P

W = 128
MODES = 4
TS = 384
GY = 4
POS = 32
NZ = 8
NY = 4
DEPTH = 8
BOTH = 2 * W
ROWS_A = 96
ROWS_B = BOTH - ROWS_A
HALF_B = ROWS_B // 2
CHUNKS = TS // W + 2
PADDED = TS + 2 * W

count_scale = 0.0078125
loss_scale = 0.03125
fresnel_strength = 40.0

VMEM = pl.BlockSpec(memory_space=pltpu.VMEM)
SMEM = pl.BlockSpec(memory_space=pltpu.SMEM)
HBM = pl.BlockSpec(memory_space=pltpu.HBM)
ANY = pl.BlockSpec(memory_space=pl.ANY)
MESH = pl.DeviceIdType.MESH


def make_tables():
    index = np.arange(W)
    angle = 2.0 * np.pi * ((index[:, None] * index[None, :]) % W) / W
    dft = np.exp(-1j * angle) / math.sqrt(W)
    signed = ((index + W // 2) % W - W // 2) / W
    chirp = np.exp(-1j * fresnel_strength * signed**2)
    step = np.conj(dft) @ (chirp[:, None] * dft)
    tables = []
    for g in (step, dft):
        right = np.block([[g.real, g.imag], [-g.imag, g.real]])
        for table in (right, right.T):
            table = table.astype(np.float32)
            high = table.astype(jnp.bfloat16)
            low = (table - high.astype(np.float32)).astype(jnp.bfloat16)
            tables.append(np.stack([high, low]))
    return np.stack(tables)


def tile_corner(slots, me):
    def look(i, place):
        return jnp.where(slots[i] == me, i, place)

    place = lax.fori_loop(0, POS, look, jnp.int32(0))
    row = lax.shift_right_logical(place, 2)
    return row * TS, (place - row * GY) * TS


def overlap(rows, cols, p, top, left):
    dr = rows[p] - top
    dc = cols[p] - left
    return dr, dc, (dr > -W) & (dr < TS) & (dc > -W) & (dc < TS)


def deposit_kernel(rows, cols, slots, grads, phase_out, absorb_out, acc, held, sems):
    me = lax.axis_index("tile")
    top, left = tile_corner(slots, me)

    z, y = tile_place()

    def fetch(p):
        row = lax.shift_right_logical(p, 2)
        place = turned(row, -z, NZ) * NY + turned(p - row * NY, -y, NY)
        return pltpu.make_async_copy(grads.at[place], held.at[p], sems.at[p])

    def begin(p, carry):
        dr, dc, touches = overlap(rows, cols, p, top, left)

        @pl.when(touches)
        def _():
            fetch(p).start()

        return carry

    lax.fori_loop(0, POS, begin, 0)
    acc[...] = jnp.zeros_like(acc)
    lane = lax.broadcasted_iota(jnp.int32, (W, W), 1)

    def one(p, carry):
        dr, dc, touches = overlap(rows, cols, p, top, left)

        @pl.when(touches)
        def _():
            fetch(p).wait()
            start = dr + W
            chunk = lax.shift_right_logical(dc + W, 7)
            shift = dc + W - chunk * W
            for m in range(2):
                moved = pltpu.roll(held[p, m * W : (m + 1) * W], shift, 1)
                acc[m, chunk, pl.ds(start, W), :] += jnp.where(lane >= shift, moved, 0.0)
                acc[m, chunk + 1, pl.ds(start, W), :] += jnp.where(lane < shift, moved, 0.0)

        return carry

    lax.fori_loop(0, POS, one, 0)
    for m, target in enumerate((phase_out, absorb_out)):
        for c in range(TS // W):
            target[0, 0, :, c * W : (c + 1) * W] = acc[m, c + 1, W : W + TS, :]


def tile_place():
    me = lax.axis_index("tile")
    z = me // NY
    return z, me - z * NY


def turned(value, step, count):
    return lax.rem(value + step + count, count)


def z_device(way):
    z, y = tile_place()
    return {"tile": turned(z, way, NZ) * NY + y}


def y_device(step):
    z, y = tile_place()
    return {"tile": z * NY + turned(y, step, NY)}


def tile_partners():
    return [z_device(k) for k in (1, -1, 2, -2)] + [y_device(k) for k in range(1, NY)]


class Sender:
    def __init__(self, send_sems, recv_sems):
        self.send_sems, self.recv_sems = send_sems, recv_sems
        self.started = []

    def copy(self, source, target, device):
        n = len(self.started)
        copy = pltpu.make_async_remote_copy(
            src_ref=source,
            dst_ref=target,
            send_sem=self.send_sems.at[n],
            recv_sem=self.recv_sems.at[n],
            device_id=device,
            device_id_type=MESH,
        )
        copy.start()
        self.started.append(copy)
        return copy

    def finish(self):
        for copy in self.started:
            copy.wait_send()


HOPS4 = ((0, 1), (1, 1), (2, -1), (3, -1))
HOPS3 = ((2, 1), (3, 1), (0, -1), (1, -1))
SCATTER_COPIES = 28 + 3 + 24 + 8
GATHER_COPIES = 28 + 3 + 24 + 8
FAR_FIRST = (4, 3, -3, 2, -2, 1, -1, 0)
PART_A = pl.ds(0, ROWS_A)
PART_B = pl.ds(ROWS_A, ROWS_B)
ALL_B = pl.ds(0, ROWS_B)


def half_of(way):
    return 0 if way == 1 else HALF_B


def spot(dz, dy):
    return (dz % NZ) * NY + dy % NY


def scatter(extract, ready, ext, out, a_recv, a_side, b_recv, b_sum, c_recv, send):
    a_last, b_last, c_last = {}, {}, {}
    a_slots, b_slots = iter(range(28)), iter(range(24))

    def a_step(streams, length, s):
        for stream, way in streams:
            dest = spot(way * (length - s), stream)
            if s > 0:
                copy, slot = a_last[stream, way]
                copy.wait_recv()
                a_recv[slot] += ext[dest, PART_A]
                source = a_recv.at[slot]
            else:
                source = ext.at[dest, PART_A]
            slot = next(a_slots)
            a_last[stream, way] = (send.copy(source, a_recv.at[slot], z_device(way)), slot)

    def b_send(offset, way, source):
        slot = next(b_slots)
        b_last[offset, way] = (send.copy(source, b_recv.at[slot], y_device(way)), slot)

    def b_far(offset):
        way = 1 if offset % 2 == 0 else -1
        b_send(offset, way, ext.at[spot(offset, 2), PART_B])
        b_send(offset, -way, ext.at[spot(offset, -way), PART_B])

    def b_near(offset):
        way = 1 if offset % 2 == 0 else -1
        copy, slot = b_last[offset, way]
        copy.wait_recv()
        b_recv[slot] += ext[spot(offset, way), PART_B]
        b_send(offset, way, b_recv.at[slot])

    def b_total(offset):
        total = ext[spot(offset, 0), PART_B]
        for way in (1, -1):
            copy, slot = b_last[offset, way]
            copy.wait_recv()
            total = total + b_recv[slot]
        b_sum[offset % NZ] = total

    def c_slot(away, way):
        return 2 * (away - 1) + (way < 0)

    def c_send(away, way, source, part, hops):
        target = c_recv.at[c_slot(away, way), part]
        c_last[away, way] = send.copy(source, target, z_device(way * hops))

    def c_far():
        for way in (1, -1):
            part = pl.ds(half_of(way), HALF_B)
            c_send(4, way, b_sum.at[4, part], part, 2)
        for way in (1, -1):
            c_send(3, way, b_sum.at[3 * way % NZ], ALL_B, 1)

    def c_two(way):
        c_last[3, way].wait_recv()
        c_last[4, way].wait_recv()
        slot = c_slot(3, way)
        part = pl.ds(half_of(way), HALF_B)
        c_recv[slot] += b_sum[2 * way % NZ]
        c_recv[slot, part] += c_recv[c_slot(4, way), part]
        c_send(2, way, c_recv.at[slot], ALL_B, 2)

    def c_one(way):
        c_send(1, way, b_sum.at[way % NZ], ALL_B, 1)

    extract(4)
    ready()
    a_step(HOPS4, 4, 0)
    b_far(4)
    extract(3)
    a_step(HOPS3[:2], 3, 0)
    extract(-3)
    a_step(HOPS3[2:], 3, 0)
    b_far(3)
    extract(2)
    extract(-2)
    b_far(-3)
    a_step(HOPS4, 4, 1)
    b_near(4)
    b_far(2)
    extract(1)
    extract(-1)
    a_step(HOPS3, 3, 1)
    b_near(3)
    b_far(-2)
    extract(0)
    a_step(HOPS4, 4, 2)
    b_near(-3)
    b_far(1)
    b_total(4)
    a_step(HOPS3, 3, 2)
    b_near(2)
    b_far(-1)
    b_total(3)
    b_total(-3)
    c_far()
    a_step(HOPS4, 4, 3)
    b_near(-2)
    b_far(0)
    b_total(2)
    b_near(1)
    b_total(-2)
    for stream in range(NY):
        total = ext[spot(0, stream), PART_A]
        for way in (1, -1):
            copy, slot = a_last[stream, way]
            copy.wait_recv()
            total = total + a_recv[slot]
        a_side[stream] = total
    a_copies = [
        send.copy(a_side.at[step], a_side.at[NY + step], y_device(step)) for step in (1, 3, 2)
    ]
    c_two(1)
    c_two(-1)
    b_near(-1)
    b_total(1)
    c_one(1)
    b_near(0)
    b_total(-1)
    c_one(-1)
    b_total(0)
    total = a_side[0]
    for step, copy in zip((1, 3, 2), a_copies):
        copy.wait_recv()
        total = total + a_side[NY + step]
    out[PART_A] = total
    total = b_sum[0]
    for away in (2, 1):
        for way in (1, -1):
            c_last[away, way].wait_recv()
            total = total + c_recv[c_slot(away, way)]
    out[PART_B] = total


def gather(out, send):
    a_last, b_last, c_last = {}, {}, {}

    def z_copy(dz, dy, part, way):
        source, target = out.at[spot(dz, dy), part], out.at[spot(dz - way, dy), part]
        return send.copy(source, target, z_device(way))

    def y_copy(dz, dy, part, way):
        source, target = out.at[spot(dz, dy), part], out.at[spot(dz, dy - way), part]
        return send.copy(source, target, y_device(way))

    def a_first():
        for step in (1, 3, 2):
            a_last[step] = y_copy(0, 0, PART_A, step)

    def a_step(s, streams):
        if s == 0:
            for stream in streams:
                if stream > 0:
                    a_last[stream].wait_recv()
        for found, length in ((HOPS4, 4), (HOPS3, 3)):
            for stream, way in found:
                if s >= length or stream not in streams:
                    continue
                if s > 0:
                    a_last[stream, way].wait_recv()
                a_last[stream, way] = z_copy(-way * s, -stream, PART_A, way)

    def c_near():
        for away in (1, 2):
            for way in (1, -1):
                c_last[away, way] = z_copy(0, 0, PART_B, way * away)

    def c_far(way):
        c_last[2, way].wait_recv()
        c_last[3, way] = z_copy(-2 * way, 0, PART_B, way)
        part = pl.ds(ROWS_A + half_of(way), HALF_B)
        c_last[4, way] = z_copy(-2 * way, 0, part, 2 * way)

    def b_first(offset):
        for way in (1, -1):
            b_last[offset, way] = y_copy(offset, 0, PART_B, way)

    def b_second(offset):
        way = 1 if offset % 2 == 0 else -1
        b_last[offset, way].wait_recv()
        b_last[offset, 2] = y_copy(offset, -way, PART_B, way)

    c_near()
    a_first()
    b_first(0)
    a_step(0, (0,))
    for way in (1, -1):
        c_last[1, way].wait_recv()
        b_first(-way)
    a_step(0, (1,))
    a_step(0, (3,))
    b_second(0)
    c_far(1)
    c_far(-1)
    b_first(-2)
    b_first(2)
    a_step(0, (2,))
    a_step(1, (0,))
    b_second(1)
    b_second(-1)
    a_step(1, (1,))
    a_step(1, (3,))
    for way in (1, -1):
        c_last[3, way].wait_recv()
        b_first(-3 * way)
    a_step(1, (2,))
    b_second(2)
    b_second(-2)
    a_step(2, (0,))
    for way in (1, -1):
        c_last[4, way].wait_recv()
    b_first(4)
    a_step(2, (1,))
    a_step(2, (3,))
    b_second(3)
    b_second(-3)
    a_step(2, (2,))
    a_step(3, (0,))
    b_second(4)
    a_step(3, (1, 3, 2))
    for offset in FAR_FIRST:
        forwarded = 1 if offset % 2 == 0 else -1
        b_last[offset, -forwarded].wait_recv()
        b_last[offset, 2].wait_recv()
    for stream, way in HOPS4 + HOPS3:
        a_last[stream, way].wait_recv()


def split(value):
    high = value.astype(jnp.bfloat16)
    low = (value - high.astype(jnp.float32)).astype(jnp.bfloat16)
    return high, low


def mxu(a, b):
    return jnp.dot(a, b, preferred_element_type=jnp.float32)


def transform(fields, tables, right, left):
    count = len(fields)
    high, low = split(jnp.concatenate([jnp.concatenate(field, 1) for field in fields], 0))
    half = mxu(high, tables[right, 0]) + (mxu(low, tables[right, 0]) + mxu(high, tables[right, 1]))
    blocks = [half[m * W : (m + 1) * W] for m in range(count)]
    half = jnp.concatenate(
        [
            jnp.concatenate([block[:, :W] for block in blocks], 1),
            jnp.concatenate([block[:, W:] for block in blocks], 1),
        ],
        0,
    )
    high, low = split(half)
    done = mxu(tables[left, 0], high) + (mxu(tables[left, 0], low) + mxu(tables[left, 1], high))
    return [(done[:W, m * W : (m + 1) * W], done[W:, m * W : (m + 1) * W]) for m in range(count)]


STEP, STEP_BACK, DFT, DFT_BACK = (0, 1), (1, 0), (2, 3), (3, 2)


def chain(trans, trans_ready, probe, counts, tables, waves, grads, grad_done):
    fields = [(probe[0, m], probe[1, m]) for m in range(MODES)]
    for j in range(DEPTH):
        trans_ready(j)
        tr, ti = trans[j, 0], trans[j, 1]
        entering = []
        for m, (real, imag) in enumerate(fields):
            waves[j, m, 0] = real
            waves[j, m, 1] = imag
            entering.append((tr * real - ti * imag, tr * imag + ti * real))
        fields = transform(entering, tables, *(STEP if j < DEPTH - 1 else DFT))
    intensity = sum(real * real + imag * imag for real, imag in fields)
    residual = intensity - count_scale * counts[0].astype(jnp.float32)
    residual = (4.0 * loss_scale) * residual
    fields = [(residual * real, residual * imag) for real, imag in fields]
    for j in reversed(range(DEPTH)):
        fields = transform(fields, tables, *(STEP_BACK if j < DEPTH - 1 else DFT_BACK))
        tr, ti = trans[j, 0], trans[j, 1]
        leaving, phase_part, absorb_part = [], 0.0, 0.0
        for m, (real, imag) in enumerate(fields):
            real, imag = tr * real + ti * imag, tr * imag - ti * real
            wr, wi = waves[j, m, 0], waves[j, m, 1]
            phase_part = phase_part + (wr * imag - wi * real)
            absorb_part = absorb_part - (wr * real + wi * imag)
            leaving.append((real, imag))
        fields = leaving
        grads[j, :W] = phase_part
        grads[j, W:] = absorb_part
        grad_done(j)


def main_kernel(
    rows_hbm, cols_hbm, slots_hbm, phase, absorb, probe_hbm, counts_hbm, tables_hbm,
    out,
    rows, cols, slots, probe, counts, tables,
    padded, ext, a_recv, a_side, b_recv, b_sum, c_recv, window,
    trans, waves, grads, got,
    load_sems, s_send, s_recv, g_send, g_recv, t_send, t_recv, d_send, d_recv,
):
    me = lax.axis_index("tile")
    d = lax.axis_index("depth")
    barrier = pltpu.get_barrier_semaphore()
    greeted = tile_partners()
    loads = [
        pltpu.make_async_copy(source, target, load_sems.at[i])
        for i, (source, target) in enumerate(
            [(rows_hbm, rows), (cols_hbm, cols), (slots_hbm, slots)]
            + [
                (tile.at[0, 0, :, pl.ds(c * W, W)], padded.at[m, c + 1, pl.ds(W, TS)])
                for m, tile in enumerate((phase, absorb))
                for c in range(TS // W)
            ]
            + [(probe_hbm, probe), (counts_hbm, counts), (tables_hbm, tables)]
        )
    ]
    for load in loads[:3]:
        load.start()
    for m in range(2):
        for c in range(CHUNKS):
            if 1 <= c <= TS // W:
                padded[m, c, :W] = jnp.zeros((W, W), jnp.float32)
                padded[m, c, W + TS :] = jnp.zeros((W, W), jnp.float32)
            else:
                padded[m, c] = jnp.zeros((PADDED, W), jnp.float32)
    for load in loads[3:9]:
        load.start()
    for partner in greeted:
        pl.semaphore_signal(barrier, inc=1, device_id=partner, device_id_type=MESH)

    @pl.when(d == 0)
    def _():
        for k in range(1, DEPTH):
            pl.semaphore_signal(barrier, inc=1, device_id={"depth": k}, device_id_type=MESH)

    @pl.when(d != 0)
    def _():
        pl.semaphore_signal(barrier, inc=1, device_id={"depth": 0}, device_id_type=MESH)

    for load in loads[:9]:
        load.wait()
    top, left = tile_corner(slots, me)
    lane = lax.broadcasted_iota(jnp.int32, (W, W), 1)
    z, y = tile_place()

    def extract_one(dz, dy):
        p = turned(z, dz, NZ) * NY + turned(y, dy, NY)
        start = jnp.clip(rows[p] - top, -W, TS) + W
        column = jnp.clip(cols[p] - left, -W, TS) + W
        chunk = lax.shift_right_logical(column, 7)
        after = jnp.minimum(chunk + 1, CHUNKS - 1)
        shift = column - chunk * W
        back = lax.bitwise_and(W - shift, W - 1)
        for m in range(2):
            first = padded[m, chunk, pl.ds(start, W), :]
            second = padded[m, after, pl.ds(start, W), :]
            ext[spot(dz, dy), m * W : (m + 1) * W] = pltpu.roll(
                jnp.where(lane >= shift, first, second), back, 1
            )

    def extract(offset):
        for dy in range(NY):
            extract_one(offset, dy)

    def ready():
        pl.semaphore_wait(barrier, len(greeted) + jnp.where(d == 0, DEPTH - 1, 1))
        for load in loads[9:]:
            load.start()

    send = Sender(s_send, s_recv)
    scatter(extract, ready, ext, window, a_recv, a_side, b_recv, b_sum, c_recv, send)

    damping = jnp.exp(-window[W:])
    trans[d, 0] = damping * jnp.cos(window[:W])
    trans[d, 1] = damping * jnp.sin(window[:W])

    def trans_copy(j, send_slot):
        return pltpu.make_async_remote_copy(
            src_ref=trans.at[j],
            dst_ref=trans.at[j],
            send_sem=t_send.at[0],
            recv_sem=t_recv.at[j],
            device_id={"depth": send_slot},
            device_id_type=MESH,
        )

    def grad_copy(j):
        return pltpu.make_async_remote_copy(
            src_ref=grads.at[j],
            dst_ref=got,
            send_sem=d_send.at[j],
            recv_sem=d_recv.at[0],
            device_id={"depth": j},
            device_id_type=MESH,
        )

    @pl.when(d == 0)
    def _():
        for load in loads[9:]:
            load.wait()

        def trans_ready(j):
            if j > 0:
                trans_copy(j, 1).wait_recv()

        def grad_done(j):
            if j > 0:
                grad_copy(j).start()
            else:
                out[0] = grads[0]

        chain(trans, trans_ready, probe, counts, tables, waves, grads, grad_done)

    @pl.when(d != 0)
    def _():
        trans_copy(d, 0).start()
        for load in loads[9:]:
            load.wait()
        trans_copy(d, 0).wait_send()
        pltpu.make_async_remote_copy(
            src_ref=got,
            dst_ref=got,
            send_sem=d_send.at[0],
            recv_sem=d_recv.at[0],
            device_id={"depth": 0},
            device_id_type=MESH,
        ).wait_recv()
        out[0] = got[...]

    send_back = Sender(g_send, g_recv)
    gather(out, send_back)

    @pl.when(d == 0)
    def _():
        for j in range(1, DEPTH):
            grad_copy(j).wait_send()

    send.finish()
    send_back.finish()


def local(phase, absorb, probe, row_offsets, col_offsets, tile_slot, counts):
    f32 = jnp.float32
    mib = 1 << 20
    dma = pltpu.SemaphoreType.DMA
    tables = jnp.asarray(make_tables())
    gathered = pl.pallas_call(
        main_kernel,
        out_shape=jax.ShapeDtypeStruct((POS, BOTH, W), f32),
        in_specs=[HBM] * 8,
        out_specs=VMEM,
        scratch_shapes=[
            pltpu.SMEM((POS,), jnp.int32),
            pltpu.SMEM((POS,), jnp.int32),
            pltpu.SMEM((POS,), jnp.int32),
            pltpu.VMEM(probe.shape, f32),
            pltpu.VMEM(counts.shape, jnp.int32),
            pltpu.VMEM(tables.shape, jnp.bfloat16),
            pltpu.VMEM((2, CHUNKS, PADDED, W), f32),
            pltpu.VMEM((POS, BOTH, W), f32),
            pltpu.VMEM((28, ROWS_A, W), f32),
            pltpu.VMEM((2 * NY, ROWS_A, W), f32),
            pltpu.VMEM((24, ROWS_B, W), f32),
            pltpu.VMEM((NZ, ROWS_B, W), f32),
            pltpu.VMEM((8, ROWS_B, W), f32),
            pltpu.VMEM((BOTH, W), f32),
            pltpu.VMEM((DEPTH, 2, W, W), f32),
            pltpu.VMEM((DEPTH, MODES, 2, W, W), f32),
            pltpu.VMEM((DEPTH, BOTH, W), f32),
            pltpu.VMEM((BOTH, W), f32),
            dma((12,)),
            dma((SCATTER_COPIES,)),
            dma((SCATTER_COPIES,)),
            dma((GATHER_COPIES,)),
            dma((GATHER_COPIES,)),
            dma((1,)),
            dma((DEPTH,)),
            dma((DEPTH,)),
            dma((1,)),
        ],
        compiler_params=pltpu.CompilerParams(
            collective_id=0, has_side_effects=True, vmem_limit_bytes=60 * mib
        ),
        name="main",
    )(row_offsets, col_offsets, tile_slot, phase, absorb, probe, counts, tables)
    return pl.pallas_call(
        deposit_kernel,
        out_shape=(jax.ShapeDtypeStruct((1, 1, TS, TS), f32),) * 2,
        in_specs=[SMEM, SMEM, SMEM, ANY],
        out_specs=(VMEM, VMEM),
        scratch_shapes=[
            pltpu.VMEM((2, TS // W + 2, PADDED, W), f32),
            pltpu.VMEM((POS, BOTH, W), f32),
            dma((POS,)),
        ],
        compiler_params=pltpu.CompilerParams(vmem_limit_bytes=60 * mib),
        name="deposit",
    )(row_offsets, col_offsets, tile_slot, gathered)


def solution(mesh):
    in_specs = (
        P("depth", "tile", None, None),
        P("depth", "tile", None, None),
        P(),
        P(),
        P(),
        P(),
        P("tile", None, None),
    )
    out_specs = (P("depth", "tile", None, None), P("depth", "tile", None, None))
    return jax.shard_map(local, mesh=mesh, in_specs=in_specs, out_specs=out_specs, check_vma=False)
```

time: 875 us -> 96.5 us (0.11); the launches traced: 864 us -> 96.4 us
  waiting for transfers between devices: 429 us -> 0 us
  local copies, waits for them, and re-layouts: 178 us -> 0 us
  Pallas kernels: 0 us -> 95.6 us
  matrix products: 78.1 us -> 0 us
  other arithmetic: 73.3 us -> 0 us
  loops' own time: 45.3 us -> 0 us
  starting transfers between devices: 43.2 us -> 0 us
  between operations: 17 us -> 0.8 us
    reduce_scatter x1 -> x0, waiting for transfers between devices: 224 us -> none  [local(): lax.psum_scatter(jax.vmap(extract)(row_offsets, col_offsets), 'tile', sca...]
    ppermute x16 -> x0, waiting for transfers between devices: 124 us -> none  [shifted(): lax.ppermute(value, axis, [(source, source + steps) for source in range(f...]
    pallas_call x0 -> x2, Pallas kernels: none -> 95.6 us  [the longest x1 91.3 us: local(): pl.pallas_call(main_kernel, out_shape=jax.ShapeDtypeStruct((POS, BOTH, W)...]
    gather x96 -> x0, local copies, waits for them, and re-layouts: 84.2 us -> none
    all_gather x1 -> x0, waiting for transfers between devices: 81.1 us -> none  [local(): part_rows = lax.all_gather(window_grads, 'tile', axis=0, tiled=True)]
    dot_general x102 -> x0, matrix products: 78.1 us -> none  [the longest x34 27.8 us: transform(): jnp.einsum('ij,...jk->...ik', sin_t, half_done, precision=lax.Precision.H...]
    dynamic_update_slice x32 -> x0, local copies, waits for them, and re-layouts: 50.5 us -> none  [add_one(): return lax.dynamic_update_slice(running, current + addend, where_at)]
    another operation x4 -> x0, loops' own time: 45.3 us -> none  [the longest x1 43 us: local(): deposit_sum = lax.fori_loop(0, part_rows.shape[0], add_one, empty_tile)]
  transfers between devices with their start and end apart: 18 -> 0, of which waited for: 18 -> 0; matrix products, arithmetic and copies ran while one was open for 0% -> 0% of each run, Pallas kernels for 0% -> 0%
where the time goes in v2:
time: 96.5 us; the launch traced here: 96.4 us
  Pallas kernels  95.6 us (99%)
    pallas_call x1, Pallas kernels, local(): pl.pallas_call(main_kernel, out_shape=jax.ShapeDtypeStruct((POS, BOTH, W)...  91.3 us
    pallas_call x1, Pallas kernels, local(): pl.pallas_call(deposit_kernel, out_shape=(jax.ShapeDtypeStruct((1, 1, TS,...  4.24 us

profile of v2, /device:TPU:2, one launch (start us, length us, event | category | flops | bytes accessed | tf_op | source)
XLA Modules:
  0.0 96.4 jit_solution(1623044338107147978)
XLA Ops:
  0.6 91.3 %main.1.grads = f32[32,256,128]{2,1,0:T(8,128)} custom-call(s32[32]{0:T(128)} %rows.1, s32[32]{0:T(128)} %cols.1, s32[32]{0:T(128)} %slots.1, f32[1,1,384,384]{3,2,1,0:T(8,128)} %phase.1, f32[1,1,384,384]{3,2,1,0:T(8,128)} %absorb.1, f32[2,4,128,128]{3,2,1,0:T(8,128)} %probe_hbm.1, s32[1,128,128]{2,1,0:T(8,128)} %counts_hbm.1, ...), custom_call_target="tpu_custom_call" | custom-call | tf_op jit(solution)/shard_map/main/pallas_call | solution.py:628
  92.0 4.2 %deposit.1 = (f32[1,1,384,384]{3,2,1,0:T(8,128)}, f32[1,1,384,384]{3,2,1,0:T(8,128)}) custom-call(s32[32]{0:T(128)} %rows.1, s32[32]{0:T(128)} %cols.1, s32[32]{0:T(128)} %slots.1, f32[32,256,128]{2,1,0:T(8,128)} %main.1.grads), custom_call_target="tpu_custom_call" | custom-call | tf_op jit(solution)/shard_map/deposit/pallas_call | solution.py:667

commit v3 on v2

--- a/solution.py
+++ b/solution.py
@@ -18,9 +18,17 @@
 NY = 4
 DEPTH = 8
 BOTH = 2 * W
-ROWS_A = 96
+PIXELS = 48
+ROWS_A = 2 * PIXELS
 ROWS_B = BOTH - ROWS_A
 HALF_B = ROWS_B // 2
+REST = W - PIXELS
+BANDS = (
+    (slice(0, PIXELS), 0, slice(0, PIXELS)),
+    (slice(PIXELS, ROWS_A), 1, slice(0, PIXELS)),
+    (slice(ROWS_A, ROWS_A + REST), 0, slice(PIXELS, W)),
+    (slice(ROWS_A + REST, BOTH), 1, slice(PIXELS, W)),
+)
 CHUNKS = TS // W + 2
 PADDED = TS + 2 * W
 
@@ -102,7 +110,8 @@
             chunk = lax.shift_right_logical(dc + W, 7)
             shift = dc + W - chunk * W
             for m in range(2):
-                moved = pltpu.roll(held[p, m * W : (m + 1) * W], shift, 1)
+                pieces = [held[p, rows_in] for rows_in, kind, _ in BANDS if kind == m]
+                moved = pltpu.roll(jnp.concatenate(pieces, 0), shift, 1)
                 acc[m, chunk, pl.ds(start, W), :] += jnp.where(lane >= shift, moved, 0.0)
                 acc[m, chunk + 1, pl.ds(start, W), :] += jnp.where(lane < shift, moved, 0.0)
 
@@ -180,7 +189,7 @@
     return (dz % NZ) * NY + dy % NY
 
 
-def scatter(extract, ready, ext, out, a_recv, a_side, b_recv, b_sum, c_recv, send):
+def scatter(extract, ready, done_a, done_b, ext, a_recv, a_side, b_recv, b_sum, c_recv, send):
     a_last, b_last, c_last = {}, {}, {}
     a_slots, b_slots = iter(range(28)), iter(range(24))
 
@@ -221,31 +230,18 @@
             total = total + b_recv[slot]
         b_sum[offset % NZ] = total
 
-    def c_slot(away, way):
-        return 2 * (away - 1) + (way < 0)
-
-    def c_send(away, way, source, part, hops):
-        target = c_recv.at[c_slot(away, way), part]
-        c_last[away, way] = send.copy(source, target, z_device(way * hops))
-
-    def c_far():
-        for way in (1, -1):
-            part = pl.ds(half_of(way), HALF_B)
-            c_send(4, way, b_sum.at[4, part], part, 2)
-        for way in (1, -1):
-            c_send(3, way, b_sum.at[3 * way % NZ], ALL_B, 1)
-
-    def c_two(way):
-        c_last[3, way].wait_recv()
-        c_last[4, way].wait_recv()
-        slot = c_slot(3, way)
-        part = pl.ds(half_of(way), HALF_B)
-        c_recv[slot] += b_sum[2 * way % NZ]
-        c_recv[slot, part] += c_recv[c_slot(4, way), part]
-        c_send(2, way, c_recv.at[slot], ALL_B, 2)
-
-    def c_one(way):
-        c_send(1, way, b_sum.at[way % NZ], ALL_B, 1)
+    def c_send(away, way):
+        slot = 2 * (away - 1) + (way < 0)
+        part = pl.ds(half_of(way), HALF_B) if away == 4 else ALL_B
+        source = b_sum.at[way * away % NZ, part]
+        if away < 4:
+            if (away + 1, way) in c_last:
+                copy, held = c_last[away + 1, way]
+                copy.wait_recv()
+                part_held = pl.ds(half_of(way), HALF_B) if away == 3 else ALL_B
+                b_sum[way * away % NZ, part_held] += c_recv[held, part_held]
+        target = c_recv.at[slot, part]
+        c_last[away, way] = (send.copy(source, target, z_device(way)), slot)
 
     extract(4)
     ready()
@@ -253,78 +249,80 @@
     b_far(4)
     extract(3)
     a_step(HOPS3[:2], 3, 0)
+    b_far(3)
     extract(-3)
     a_step(HOPS3[2:], 3, 0)
-    b_far(3)
+    b_near(4)
+    b_far(-3)
     extract(2)
     extract(-2)
-    b_far(-3)
     a_step(HOPS4, 4, 1)
-    b_near(4)
+    b_near(3)
     b_far(2)
     extract(1)
     extract(-1)
+    b_total(4)
+    c_send(4, 1)
+    c_send(4, -1)
     a_step(HOPS3, 3, 1)
-    b_near(3)
+    b_near(-3)
     b_far(-2)
     extract(0)
+    b_total(3)
+    c_send(3, 1)
     a_step(HOPS4, 4, 2)
-    b_near(-3)
+    b_near(2)
     b_far(1)
-    b_total(4)
+    b_total(-3)
+    c_send(3, -1)
     a_step(HOPS3, 3, 2)
-    b_near(2)
+    b_near(-2)
     b_far(-1)
-    b_total(3)
-    b_total(-3)
-    c_far()
+    b_total(2)
+    c_send(2, 1)
     a_step(HOPS4, 4, 3)
-    b_near(-2)
+    b_near(1)
     b_far(0)
-    b_total(2)
-    b_near(1)
     b_total(-2)
-    for stream in range(NY):
+    c_send(2, -1)
+    for stream in (1, 3, 2, 0):
         total = ext[spot(0, stream), PART_A]
         for way in (1, -1):
             copy, slot = a_last[stream, way]
             copy.wait_recv()
             total = total + a_recv[slot]
         a_side[stream] = total
-    a_copies = [
-        send.copy(a_side.at[step], a_side.at[NY + step], y_device(step)) for step in (1, 3, 2)
-    ]
-    c_two(1)
-    c_two(-1)
+        if stream > 0:
+            a_last[stream] = send.copy(a_side.at[stream], a_side.at[NY + stream], y_device(stream))
     b_near(-1)
     b_total(1)
-    c_one(1)
+    c_send(1, 1)
     b_near(0)
     b_total(-1)
-    c_one(-1)
+    c_send(1, -1)
+    total = a_side[0]
+    for stream in (1, 3, 2):
+        a_last[stream].wait_recv()
+        total = total + a_side[NY + stream]
+    done_a(total)
     b_total(0)
-    total = a_side[0]
-    for step, copy in zip((1, 3, 2), a_copies):
+    total = b_sum[0]
+    for way in (1, -1):
+        copy, slot = c_last[1, way]
         copy.wait_recv()
-        total = total + a_side[NY + step]
-    out[PART_A] = total
-    total = b_sum[0]
-    for away in (2, 1):
-        for way in (1, -1):
-            c_last[away, way].wait_recv()
-            total = total + c_recv[c_slot(away, way)]
-    out[PART_B] = total
-
-
-def gather(out, send):
+        total = total + c_recv[slot]
+    done_b(total)
+
+
+def gather(held, keep, send):
     a_last, b_last, c_last = {}, {}, {}
 
     def z_copy(dz, dy, part, way):
-        source, target = out.at[spot(dz, dy), part], out.at[spot(dz - way, dy), part]
+        source, target = held.at[spot(dz, dy), part], held.at[spot(dz - way, dy), part]
         return send.copy(source, target, z_device(way))
 
     def y_copy(dz, dy, part, way):
-        source, target = out.at[spot(dz, dy), part], out.at[spot(dz, dy - way), part]
+        source, target = held.at[spot(dz, dy), part], held.at[spot(dz, dy - way), part]
         return send.copy(source, target, y_device(way))
 
     def a_first():
@@ -336,78 +334,90 @@
             for stream in streams:
                 if stream > 0:
                     a_last[stream].wait_recv()
+                    keep(0, -stream, PART_A)
         for found, length in ((HOPS4, 4), (HOPS3, 3)):
             for stream, way in found:
-                if s >= length or stream not in streams:
+                if s > length or stream not in streams:
                     continue
                 if s > 0:
                     a_last[stream, way].wait_recv()
-                a_last[stream, way] = z_copy(-way * s, -stream, PART_A, way)
-
-    def c_near():
-        for away in (1, 2):
-            for way in (1, -1):
-                c_last[away, way] = z_copy(0, 0, PART_B, way * away)
-
-    def c_far(way):
-        c_last[2, way].wait_recv()
-        c_last[3, way] = z_copy(-2 * way, 0, PART_B, way)
-        part = pl.ds(ROWS_A + half_of(way), HALF_B)
-        c_last[4, way] = z_copy(-2 * way, 0, part, 2 * way)
+                    keep(-way * s, -stream, PART_A)
+                if s < length:
+                    a_last[stream, way] = z_copy(-way * s, -stream, PART_A, way)
+
+    def c_send(away, way):
+        part = pl.ds(ROWS_A + half_of(way), HALF_B) if away == 4 else PART_B
+        if away > 1:
+            c_last[away - 1, way].wait_recv()
+        c_last[away, way] = z_copy(-way * (away - 1), 0, part, way)
 
     def b_first(offset):
         for way in (1, -1):
             b_last[offset, way] = y_copy(offset, 0, PART_B, way)
+        if offset != 0:
+            keep(offset, 0, PART_B)
 
     def b_second(offset):
         way = 1 if offset % 2 == 0 else -1
         b_last[offset, way].wait_recv()
         b_last[offset, 2] = y_copy(offset, -way, PART_B, way)
-
-    c_near()
+        keep(offset, -way, PART_B)
+
+    def b_last_two(offset):
+        way = 1 if offset % 2 == 0 else -1
+        b_last[offset, -way].wait_recv()
+        keep(offset, way, PART_B)
+        b_last[offset, 2].wait_recv()
+        keep(offset, 2, PART_B)
+
+    c_send(1, 1)
+    c_send(1, -1)
     a_first()
     b_first(0)
     a_step(0, (0,))
     for way in (1, -1):
-        c_last[1, way].wait_recv()
+        c_send(2, way)
         b_first(-way)
+    keep(0, 0, pl.ds(0, BOTH))
     a_step(0, (1,))
     a_step(0, (3,))
     b_second(0)
-    c_far(1)
-    c_far(-1)
-    b_first(-2)
-    b_first(2)
     a_step(0, (2,))
+    for way in (1, -1):
+        c_send(3, way)
+        b_first(-2 * way)
     a_step(1, (0,))
     b_second(1)
     b_second(-1)
     a_step(1, (1,))
     a_step(1, (3,))
     for way in (1, -1):
-        c_last[3, way].wait_recv()
+        c_send(4, way)
         b_first(-3 * way)
     a_step(1, (2,))
+    b_last_two(0)
     b_second(2)
     b_second(-2)
     a_step(2, (0,))
+    a_step(2, (1,))
+    a_step(2, (3,))
     for way in (1, -1):
         c_last[4, way].wait_recv()
     b_first(4)
-    a_step(2, (1,))
-    a_step(2, (3,))
+    b_last_two(1)
+    b_last_two(-1)
+    a_step(2, (2,))
     b_second(3)
     b_second(-3)
-    a_step(2, (2,))
     a_step(3, (0,))
+    b_last_two(2)
+    b_last_two(-2)
+    a_step(3, (1, 3, 2))
     b_second(4)
-    a_step(3, (1, 3, 2))
-    for offset in FAR_FIRST:
-        forwarded = 1 if offset % 2 == 0 else -1
-        b_last[offset, -forwarded].wait_recv()
-        b_last[offset, 2].wait_recv()
-    for stream, way in HOPS4 + HOPS3:
-        a_last[stream, way].wait_recv()
+    a_step(4, (0, 1, 3, 2))
+    b_last_two(3)
+    b_last_two(-3)
+    b_last_two(4)
 
 
 def split(value):
@@ -421,20 +431,20 @@
 
 
 def transform(fields, tables, right, left):
-    count = len(fields)
-    high, low = split(jnp.concatenate([jnp.concatenate(field, 1) for field in fields], 0))
-    half = mxu(high, tables[right, 0]) + (mxu(low, tables[right, 0]) + mxu(high, tables[right, 1]))
-    blocks = [half[m * W : (m + 1) * W] for m in range(count)]
-    half = jnp.concatenate(
-        [
-            jnp.concatenate([block[:, :W] for block in blocks], 1),
-            jnp.concatenate([block[:, W:] for block in blocks], 1),
-        ],
-        0,
-    )
-    high, low = split(half)
-    done = mxu(tables[left, 0], high) + (mxu(tables[left, 0], low) + mxu(tables[left, 1], high))
-    return [(done[:W, m * W : (m + 1) * W], done[W:, m * W : (m + 1) * W]) for m in range(count)]
+    halves = []
+    for field in fields:
+        high, low = split(jnp.concatenate(field, 1))
+        halves.append(
+            mxu(high, tables[right, 0])
+            + (mxu(low, tables[right, 0]) + mxu(high, tables[right, 1]))
+        )
+    done = []
+    for half in halves:
+        high, low = split(jnp.concatenate([half[:, :W], half[:, W:]], 0))
+        both = mxu(tables[left, 0], jnp.concatenate([high, low], 1))
+        whole = both[:, :W] + (both[:, W:] + mxu(tables[left, 1], high))
+        done.append((whole[:W], whole[W:]))
+    return done
 
 
 STEP, STEP_BACK, DFT, DFT_BACK = (0, 1), (1, 0), (2, 3), (3, 2)
@@ -466,8 +476,8 @@
             absorb_part = absorb_part - (wr * real + wi * imag)
             leaving.append((real, imag))
         fields = leaving
-        grads[j, :W] = phase_part
-        grads[j, W:] = absorb_part
+        for rows_in, kind, rows_of in BANDS:
+            grads[j, rows_in] = (phase_part, absorb_part)[kind][rows_of]
         grad_done(j)
 
 
@@ -475,9 +485,9 @@
     rows_hbm, cols_hbm, slots_hbm, phase, absorb, probe_hbm, counts_hbm, tables_hbm,
     out,
     rows, cols, slots, probe, counts, tables,
-    padded, ext, a_recv, a_side, b_recv, b_sum, c_recv, window,
+    padded, ext, a_recv, a_side, b_recv, b_sum, c_recv, held,
     trans, waves, grads, got,
-    load_sems, s_send, s_recv, g_send, g_recv, t_send, t_recv, d_send, d_recv,
+    load_sems, s_send, s_recv, g_send, g_recv, t_send, t_recv, d_send, d_recv, keep_sems,
 ):
     me = lax.axis_index("tile")
     d = lax.axis_index("depth")
@@ -535,9 +545,10 @@
         for m in range(2):
             first = padded[m, chunk, pl.ds(start, W), :]
             second = padded[m, after, pl.ds(start, W), :]
-            ext[spot(dz, dy), m * W : (m + 1) * W] = pltpu.roll(
-                jnp.where(lane >= shift, first, second), back, 1
-            )
+            moved = pltpu.roll(jnp.where(lane >= shift, first, second), back, 1)
+            for rows_in, kind, rows_of in BANDS:
+                if kind == m:
+                    ext[spot(dz, dy), rows_in] = moved[rows_of]
 
     def extract(offset):
         for dy in range(NY):
@@ -549,21 +560,35 @@
             load.start()
 
     send = Sender(s_send, s_recv)
-    scatter(extract, ready, ext, window, a_recv, a_side, b_recv, b_sum, c_recv, send)
-
-    damping = jnp.exp(-window[W:])
-    trans[d, 0] = damping * jnp.cos(window[:W])
-    trans[d, 1] = damping * jnp.sin(window[:W])
-
-    def trans_copy(j, send_slot):
+
+    def trans_copy(j, part):
+        rows_of = pl.ds(0, PIXELS) if part == 0 else pl.ds(PIXELS, REST)
         return pltpu.make_async_remote_copy(
-            src_ref=trans.at[j],
-            dst_ref=trans.at[j],
-            send_sem=t_send.at[0],
-            recv_sem=t_recv.at[j],
-            device_id={"depth": send_slot},
+            src_ref=trans.at[j, :, rows_of],
+            dst_ref=trans.at[j, :, rows_of],
+            send_sem=t_send.at[part],
+            recv_sem=t_recv.at[part, j],
+            device_id={"depth": 0},
             device_id_type=MESH,
         )
+
+    def done(part):
+        def put(total):
+            rows_of = slice(0, PIXELS) if part == 0 else slice(PIXELS, W)
+            count = total.shape[0] // 2
+            damping = jnp.exp(-total[count:])
+            trans[d, 0, rows_of] = damping * jnp.cos(total[:count])
+            trans[d, 1, rows_of] = damping * jnp.sin(total[:count])
+
+            @pl.when(d != 0)
+            def _():
+                trans_copy(d, part).start()
+
+        return put
+
+    scatter(
+        extract, ready, done(0), done(1), ext, a_recv, a_side, b_recv, b_sum, c_recv, send
+    )
 
     def grad_copy(j):
         return pltpu.make_async_remote_copy(
@@ -582,22 +607,30 @@
 
         def trans_ready(j):
             if j > 0:
-                trans_copy(j, 1).wait_recv()
+                for part in range(2):
+                    pltpu.make_async_remote_copy(
+                        src_ref=trans.at[j, :, pl.ds(part * PIXELS, (PIXELS, REST)[part])],
+                        dst_ref=trans.at[j, :, pl.ds(part * PIXELS, (PIXELS, REST)[part])],
+                        send_sem=t_send.at[part],
+                        recv_sem=t_recv.at[part, j],
+                        device_id={"depth": 1},
+                        device_id_type=MESH,
+                    ).wait_recv()
 
         def grad_done(j):
             if j > 0:
                 grad_copy(j).start()
             else:
-                out[0] = grads[0]
+                held[0] = grads[0]
 
         chain(trans, trans_ready, probe, counts, tables, waves, grads, grad_done)
 
     @pl.when(d != 0)
     def _():
-        trans_copy(d, 0).start()
         for load in loads[9:]:
             load.wait()
-        trans_copy(d, 0).wait_send()
+        for part in range(2):
+            trans_copy(d, part).wait_send()
         pltpu.make_async_remote_copy(
             src_ref=got,
             dst_ref=got,
@@ -606,10 +639,20 @@
             device_id={"depth": 0},
             device_id_type=MESH,
         ).wait_recv()
-        out[0] = got[...]
+        held[0] = got[...]
 
     send_back = Sender(g_send, g_recv)
-    gather(out, send_back)
+    kept = []
+
+    def keep(dz, dy, part):
+        place = spot(dz, dy)
+        copy = pltpu.make_async_copy(
+            held.at[place, part], out.at[place, part], keep_sems.at[len(kept)]
+        )
+        copy.start()
+        kept.append(copy)
+
+    gather(held, keep, send_back)
 
     @pl.when(d == 0)
     def _():
@@ -618,6 +661,8 @@
 
     send.finish()
     send_back.finish()
+    for copy in kept:
+        copy.wait()
 
 
 def local(phase, absorb, probe, row_offsets, col_offsets, tile_slot, counts):
@@ -629,7 +674,7 @@
         main_kernel,
         out_shape=jax.ShapeDtypeStruct((POS, BOTH, W), f32),
         in_specs=[HBM] * 8,
-        out_specs=VMEM,
+        out_specs=HBM,
         scratch_shapes=[
             pltpu.SMEM((POS,), jnp.int32),
             pltpu.SMEM((POS,), jnp.int32),
@@ -644,7 +689,7 @@
             pltpu.VMEM((24, ROWS_B, W), f32),
             pltpu.VMEM((NZ, ROWS_B, W), f32),
             pltpu.VMEM((8, ROWS_B, W), f32),
-            pltpu.VMEM((BOTH, W), f32),
+            pltpu.VMEM((POS, BOTH, W), f32),
             pltpu.VMEM((DEPTH, 2, W, W), f32),
             pltpu.VMEM((DEPTH, MODES, 2, W, W), f32),
             pltpu.VMEM((DEPTH, BOTH, W), f32),
@@ -654,10 +699,11 @@
             dma((SCATTER_COPIES,)),
             dma((GATHER_COPIES,)),
             dma((GATHER_COPIES,)),
-            dma((1,)),
-            dma((DEPTH,)),
+            dma((2,)),
+            dma((2, DEPTH)),
             dma((DEPTH,)),
             dma((1,)),
+            dma((2 * POS,)),
         ],
         compiler_params=pltpu.CompilerParams(
             collective_id=0, has_side_effects=True, vmem_limit_bytes=60 * mib

time: 96.5 us -> 93.5 us (0.969)
  Pallas kernels: 95.6 us -> 92.6 us
    pallas_call x1, Pallas kernels: 91.3 us -> 88.6 us  [local(): pl.pallas_call(main_kernel, out_shape=jax.ShapeDtypeStruct((POS, BOTH, W)...]
where the time goes in v3:
time: 93.5 us; the launch traced here: 93.4 us
  Pallas kernels  92.6 us (99%)
    pallas_call x1, Pallas kernels, local(): pl.pallas_call(main_kernel, out_shape=jax.ShapeDtypeStruct((POS, BOTH, W)...  88.6 us
    pallas_call x1, Pallas kernels, local(): pl.pallas_call(deposit_kernel, out_shape=(jax.ShapeDtypeStruct((1, 1, TS,...  4.03 us

profile of v3, /device:TPU:2, one launch (start us, length us, event | category | flops | bytes accessed | tf_op | source)
XLA Modules:
  0.0 93.4 jit_solution(379840011963467454)
XLA Ops:
  0.6 88.6 %main.1.grads = f32[32,256,128]{2,1,0:T(8,128)} custom-call(s32[32]{0:T(128)} %rows.1, s32[32]{0:T(128)} %cols.1, s32[32]{0:T(128)} %slots.1, f32[1,1,384,384]{3,2,1,0:T(8,128)} %phase.1, f32[1,1,384,384]{3,2,1,0:T(8,128)} %absorb.1, f32[2,4,128,128]{3,2,1,0:T(8,128)} %probe_hbm.1, s32[1,128,128]{2,1,0:T(8,128)} %counts_hbm.1, ...), custom_call_target="tpu_custom_call" | custom-call | tf_op jit(solution)/shard_map/main/pallas_call | solution.py:673
  89.2 4.0 %deposit.1 = (f32[1,1,384,384]{3,2,1,0:T(8,128)}, f32[1,1,384,384]{3,2,1,0:T(8,128)}) custom-call(s32[32]{0:T(128)} %rows.1, s32[32]{0:T(128)} %cols.1, s32[32]{0:T(128)} %slots.1, f32[32,256,128]{2,1,0:T(8,128)} %main.1.grads), custom_call_target="tpu_custom_call" | custom-call | tf_op jit(solution)/shard_map/deposit/pallas_call | solution.py:713

commit v4 on v3

--- a/solution.py
+++ b/solution.py
@@ -18,7 +18,7 @@
 NY = 4
 DEPTH = 8
 BOTH = 2 * W
-PIXELS = 48
+PIXELS = 56
 ROWS_A = 2 * PIXELS
 ROWS_B = BOTH - ROWS_A
 HALF_B = ROWS_B // 2
@@ -171,11 +171,44 @@
             copy.wait_send()
 
 
-HOPS4 = ((0, 1), (1, 1), (2, -1), (3, -1))
-HOPS3 = ((2, 1), (3, 1), (0, -1), (1, -1))
+HOPS = {
+    (0, 1): 4, (1, 1): 4, (2, -1): 4, (3, -1): 4, (2, 1): 3, (3, 1): 3, (0, -1): 3, (1, -1): 3,
+}
+SCATTER_ORDER = (
+    ("cut", 4, 1), ("cut", 4, 3), ("cut", 4, 2), ("far", 4), ("cut", 3, 2), ("a", 1, 1, 0),
+    ("a", 3, -1, 0), ("cut", -1, 2), ("a", 2, 1, 0), ("cut", -3, 0), ("cut", -3, 2),
+    ("cut", 3, 1), ("a", 2, -1, 0), ("cut", -2, 3), ("cut", -3, 1), ("far", 3), ("cut", 3, 3),
+    ("cut", -2, 1), ("far", -3), ("cut", 4, 0), ("cut", -1, 0), ("a", 3, 1, 0), ("cut", -1, 3),
+    ("a", 1, -1, 0), ("cut", 3, 0), ("cut", 1, 1), ("a", 0, 1, 0), ("cut", 0, 2), ("cut", -2, 0),
+    ("a", 0, -1, 0), ("cut", -2, 2), ("near", 4), ("cut", -3, 3), ("cut", 2, 0), ("a", 1, 1, 1),
+    ("cut", 0, 1), ("cut", 2, 1), ("cut", 1, 2), ("far", -2), ("a", 2, -1, 1), ("cut", 2, 3),
+    ("cut", 0, 3), ("a", 1, -1, 1), ("near", -3), ("a", 3, 1, 1), ("a", 3, -1, 1), ("cut", 2, 2),
+    ("a", 0, -1, 1), ("a", 0, 1, 1), ("a", 1, 1, 2), ("far", 2), ("sum", 4), ("near", 3),
+    ("c", 4, 1), ("a", 2, 1, 1), ("near", -2), ("cut", -1, 1), ("a", 2, -1, 2), ("c", 4, -1),
+    ("far", -1), ("sum", -3), ("near", 2), ("a", 3, -1, 2), ("cut", 1, 3), ("a", 3, 1, 2),
+    ("cut", 0, 0), ("a", 1, -1, 2), ("far", 0), ("a", 1, 1, 3), ("c", 3, -1), ("sum", 3),
+    ("c", 3, 1), ("far", 1), ("a", 3, -1, 3), ("a", 2, 1, 2), ("near", -1), ("a", 2, -1, 3),
+    ("side", 1), ("sum", -2), ("a", 0, 1, 2), ("c", 2, -1), ("sum", 2), ("near", 1), ("c", 2, 1),
+    ("near", 0), ("side", 3), ("a", 0, -1, 2), ("sum", -1), ("cut", 1, 0), ("a", 0, 1, 3),
+    ("side", 2), ("sum", 1), ("c", 1, -1), ("c", 1, 1), ("sum", 0), ("side", 0), ("done_a",),
+    ("done_b",),
+)
+GATHER_ORDER = (
+    ("c", 1, 1), ("c", 1, -1), ("a_first",), ("first", 0), ("a", 0, -1, 0), ("a", 0, 1, 0),
+    ("c", 2, 1), ("first", -1), ("c", 2, -1), ("a", 2, 1, 0), ("a", 0, -1, 1), ("a", 3, -1, 0),
+    ("a", 0, 1, 1), ("first", -2), ("second", 0), ("c", 3, 1), ("a", 2, -1, 0), ("first", 2),
+    ("first", 1), ("a", 1, 1, 0), ("c", 3, -1), ("second", -1), ("a", 3, -1, 1), ("a", 2, 1, 1),
+    ("a", 3, 1, 0), ("a", 2, -1, 1), ("a", 1, -1, 0), ("a", 0, 1, 2), ("first", -3),
+    ("a", 1, 1, 1), ("a", 3, -1, 2), ("c", 4, 1), ("first", 3), ("c", 4, -1), ("a", 3, 1, 1),
+    ("a", 2, -1, 2), ("second", 1), ("second", 2), ("a", 2, 1, 2), ("end", -1), ("a", 1, -1, 1),
+    ("a", 1, 1, 2), ("first", 4), ("a", 0, -1, 2), ("second", 3), ("a", 3, 1, 2), ("a", 0, 1, 3),
+    ("second", -2), ("a", 3, -1, 3), ("a", 1, -1, 2), ("end", 2), ("end", 0), ("end", 1),
+    ("second", -3), ("a", 2, -1, 3), ("a", 1, 1, 3), ("second", 4), ("a_end", 0, 1), ("end", 3),
+    ("end", -2), ("a_end", 0, -1), ("a_end", 3, 1), ("a_end", 3, -1), ("end", -3),
+    ("a_end", 1, -1), ("a_end", 2, 1), ("a_end", 1, 1), ("end", 4), ("a_end", 2, -1),
+)
 SCATTER_COPIES = 28 + 3 + 24 + 8
 GATHER_COPIES = 28 + 3 + 24 + 8
-FAR_FIRST = (4, 3, -3, 2, -2, 1, -1, 0)
 PART_A = pl.ds(0, ROWS_A)
 PART_B = pl.ds(ROWS_A, ROWS_B)
 ALL_B = pl.ds(0, ROWS_B)
@@ -189,133 +222,115 @@
     return (dz % NZ) * NY + dy % NY
 
 
-def scatter(extract, ready, done_a, done_b, ext, a_recv, a_side, b_recv, b_sum, c_recv, send):
-    a_last, b_last, c_last = {}, {}, {}
-    a_slots, b_slots = iter(range(28)), iter(range(24))
-
-    def a_step(streams, length, s):
-        for stream, way in streams:
-            dest = spot(way * (length - s), stream)
-            if s > 0:
-                copy, slot = a_last[stream, way]
-                copy.wait_recv()
-                a_recv[slot] += ext[dest, PART_A]
-                source = a_recv.at[slot]
-            else:
-                source = ext.at[dest, PART_A]
-            slot = next(a_slots)
-            a_last[stream, way] = (send.copy(source, a_recv.at[slot], z_device(way)), slot)
-
-    def b_send(offset, way, source):
-        slot = next(b_slots)
-        b_last[offset, way] = (send.copy(source, b_recv.at[slot], y_device(way)), slot)
+class Arrivals:
+    def __init__(self):
+        self.copies, self.seen = {}, set()
+
+    def __setitem__(self, key, copy):
+        self.copies[key] = copy
+
+    def wait(self, key):
+        if key not in self.seen:
+            self.copies[key].wait_recv()
+            self.seen.add(key)
+            return True
+        return False
+
+
+def scatter(cut, ready, done_a, done_b, ext, a_recv, a_side, b_recv, b_sum, c_recv, send):
+    arrivals = Arrivals()
+    slots = {}
+
+    def take(kind, key):
+        used = slots.setdefault(kind, {})
+        used[key] = len(used)
+        return used[key]
+
+    def a_step(stream, way, s):
+        dest = spot(way * (HOPS[stream, way] - s), stream)
+        if s > 0:
+            arrivals.wait(("a", stream, way, s - 1))
+            held = slots["a"][stream, way, s - 1]
+            a_recv[held] += ext[dest, PART_A]
+            source = a_recv.at[held]
+        else:
+            source = ext.at[dest, PART_A]
+        target = a_recv.at[take("a", (stream, way, s))]
+        arrivals["a", stream, way, s] = send.copy(source, target, z_device(way))
+
+    def a_sum(stream):
+        total = ext[spot(0, stream), PART_A]
+        for way in (1, -1):
+            last = (stream, way, HOPS[stream, way] - 1)
+            arrivals.wait(("a",) + last)
+            total = total + a_recv[slots["a"][last]]
+        a_side[stream] = total
+        if stream > 0:
+            source, target = a_side.at[stream], a_side.at[NY + stream]
+            arrivals["side", stream] = send.copy(source, target, y_device(stream))
+
+    def finish_a():
+        total = a_side[0]
+        for stream in (1, 3, 2):
+            arrivals.wait(("side", stream))
+            total = total + a_side[NY + stream]
+        done_a(total)
+
+    def b_send(offset, way, step, source):
+        target = b_recv.at[take("b", (offset, way, step))]
+        arrivals["b", offset, way, step] = send.copy(source, target, y_device(way))
 
     def b_far(offset):
         way = 1 if offset % 2 == 0 else -1
-        b_send(offset, way, ext.at[spot(offset, 2), PART_B])
-        b_send(offset, -way, ext.at[spot(offset, -way), PART_B])
+        b_send(offset, way, 0, ext.at[spot(offset, 2), PART_B])
+        b_send(offset, -way, 0, ext.at[spot(offset, -way), PART_B])
 
     def b_near(offset):
         way = 1 if offset % 2 == 0 else -1
-        copy, slot = b_last[offset, way]
-        copy.wait_recv()
-        b_recv[slot] += ext[spot(offset, way), PART_B]
-        b_send(offset, way, b_recv.at[slot])
+        arrivals.wait(("b", offset, way, 0))
+        held = slots["b"][offset, way, 0]
+        b_recv[held] += ext[spot(offset, way), PART_B]
+        b_send(offset, way, 1, b_recv.at[held])
 
     def b_total(offset):
+        way = 1 if offset % 2 == 0 else -1
         total = ext[spot(offset, 0), PART_B]
-        for way in (1, -1):
-            copy, slot = b_last[offset, way]
-            copy.wait_recv()
-            total = total + b_recv[slot]
+        for key in ((offset, way, 1), (offset, -way, 0)):
+            arrivals.wait(("b",) + key)
+            total = total + b_recv[slots["b"][key]]
         b_sum[offset % NZ] = total
 
-    def c_send(away, way):
+    def c_step(away, way):
         slot = 2 * (away - 1) + (way < 0)
         part = pl.ds(half_of(way), HALF_B) if away == 4 else ALL_B
-        source = b_sum.at[way * away % NZ, part]
         if away < 4:
-            if (away + 1, way) in c_last:
-                copy, held = c_last[away + 1, way]
-                copy.wait_recv()
-                part_held = pl.ds(half_of(way), HALF_B) if away == 3 else ALL_B
-                b_sum[way * away % NZ, part_held] += c_recv[held, part_held]
-        target = c_recv.at[slot, part]
-        c_last[away, way] = (send.copy(source, target, z_device(way)), slot)
-
-    extract(4)
-    ready()
-    a_step(HOPS4, 4, 0)
-    b_far(4)
-    extract(3)
-    a_step(HOPS3[:2], 3, 0)
-    b_far(3)
-    extract(-3)
-    a_step(HOPS3[2:], 3, 0)
-    b_near(4)
-    b_far(-3)
-    extract(2)
-    extract(-2)
-    a_step(HOPS4, 4, 1)
-    b_near(3)
-    b_far(2)
-    extract(1)
-    extract(-1)
-    b_total(4)
-    c_send(4, 1)
-    c_send(4, -1)
-    a_step(HOPS3, 3, 1)
-    b_near(-3)
-    b_far(-2)
-    extract(0)
-    b_total(3)
-    c_send(3, 1)
-    a_step(HOPS4, 4, 2)
-    b_near(2)
-    b_far(1)
-    b_total(-3)
-    c_send(3, -1)
-    a_step(HOPS3, 3, 2)
-    b_near(-2)
-    b_far(-1)
-    b_total(2)
-    c_send(2, 1)
-    a_step(HOPS4, 4, 3)
-    b_near(1)
-    b_far(0)
-    b_total(-2)
-    c_send(2, -1)
-    for stream in (1, 3, 2, 0):
-        total = ext[spot(0, stream), PART_A]
+            arrivals.wait(("c", away + 1, way))
+            part_held = pl.ds(half_of(way), HALF_B) if away == 3 else ALL_B
+            b_sum[way * away % NZ, part_held] += c_recv[slot + 2, part_held]
+        source, target = b_sum.at[way * away % NZ, part], c_recv.at[slot, part]
+        arrivals["c", away, way] = send.copy(source, target, z_device(way))
+
+    def finish_b():
+        total = b_sum[0]
         for way in (1, -1):
-            copy, slot = a_last[stream, way]
-            copy.wait_recv()
-            total = total + a_recv[slot]
-        a_side[stream] = total
-        if stream > 0:
-            a_last[stream] = send.copy(a_side.at[stream], a_side.at[NY + stream], y_device(stream))
-    b_near(-1)
-    b_total(1)
-    c_send(1, 1)
-    b_near(0)
-    b_total(-1)
-    c_send(1, -1)
-    total = a_side[0]
-    for stream in (1, 3, 2):
-        a_last[stream].wait_recv()
-        total = total + a_side[NY + stream]
-    done_a(total)
-    b_total(0)
-    total = b_sum[0]
-    for way in (1, -1):
-        copy, slot = c_last[1, way]
-        copy.wait_recv()
-        total = total + c_recv[slot]
-    done_b(total)
+            arrivals.wait(("c", 1, way))
+            total = total + c_recv[(way < 0) + 0]
+        done_b(total)
+
+    steps = {
+        "cut": cut, "a": a_step, "side": a_sum, "done_a": finish_a, "far": b_far,
+        "near": b_near, "sum": b_total, "c": c_step, "done_b": finish_b,
+    }
+    waiting = True
+    for name, *which in SCATTER_ORDER:
+        if waiting and name != "cut":
+            ready()
+            waiting = False
+        steps[name](*which)
 
 
 def gather(held, keep, send):
-    a_last, b_last, c_last = {}, {}, {}
+    arrivals = Arrivals()
 
     def z_copy(dz, dy, part, way):
         source, target = held.at[spot(dz, dy), part], held.at[spot(dz - way, dy), part]
@@ -327,97 +342,60 @@
 
     def a_first():
         for step in (1, 3, 2):
-            a_last[step] = y_copy(0, 0, PART_A, step)
-
-    def a_step(s, streams):
-        if s == 0:
-            for stream in streams:
-                if stream > 0:
-                    a_last[stream].wait_recv()
-                    keep(0, -stream, PART_A)
-        for found, length in ((HOPS4, 4), (HOPS3, 3)):
-            for stream, way in found:
-                if s > length or stream not in streams:
-                    continue
-                if s > 0:
-                    a_last[stream, way].wait_recv()
-                    keep(-way * s, -stream, PART_A)
-                if s < length:
-                    a_last[stream, way] = z_copy(-way * s, -stream, PART_A, way)
-
-    def c_send(away, way):
+            arrivals["side", step] = y_copy(0, 0, PART_A, step)
+
+    def a_step(stream, way, s):
+        if s > 0:
+            arrivals.wait(("a", stream, way, s - 1))
+        elif stream > 0:
+            fresh = arrivals.wait(("side", stream))
+        arrivals["a", stream, way, s] = z_copy(-way * s, -stream, PART_A, way)
+        if s > 0 or (stream > 0 and fresh):
+            keep(-way * s, -stream, PART_A)
+
+    def a_end(stream, way):
+        hops = HOPS[stream, way]
+        arrivals.wait(("a", stream, way, hops - 1))
+        keep(-way * hops, -stream, PART_A)
+
+    def c_step(away, way):
         part = pl.ds(ROWS_A + half_of(way), HALF_B) if away == 4 else PART_B
         if away > 1:
-            c_last[away - 1, way].wait_recv()
-        c_last[away, way] = z_copy(-way * (away - 1), 0, part, way)
+            arrivals.wait(("c", away - 1, way))
+        arrivals["c", away, way] = z_copy(-way * (away - 1), 0, part, way)
 
     def b_first(offset):
+        if offset == 4:
+            arrivals.wait(("c", 4, 1))
+            arrivals.wait(("c", 4, -1))
+        elif offset != 0:
+            arrivals.wait(("c", abs(offset), 1 if offset < 0 else -1))
         for way in (1, -1):
-            b_last[offset, way] = y_copy(offset, 0, PART_B, way)
+            arrivals["b", offset, way] = y_copy(offset, 0, PART_B, way)
         if offset != 0:
             keep(offset, 0, PART_B)
 
     def b_second(offset):
         way = 1 if offset % 2 == 0 else -1
-        b_last[offset, way].wait_recv()
-        b_last[offset, 2] = y_copy(offset, -way, PART_B, way)
+        arrivals.wait(("b", offset, way))
+        arrivals["b", offset, 2] = y_copy(offset, -way, PART_B, way)
         keep(offset, -way, PART_B)
 
-    def b_last_two(offset):
+    def b_end(offset):
         way = 1 if offset % 2 == 0 else -1
-        b_last[offset, -way].wait_recv()
+        arrivals.wait(("b", offset, -way))
         keep(offset, way, PART_B)
-        b_last[offset, 2].wait_recv()
+        arrivals.wait(("b", offset, 2))
         keep(offset, 2, PART_B)
 
-    c_send(1, 1)
-    c_send(1, -1)
-    a_first()
-    b_first(0)
-    a_step(0, (0,))
-    for way in (1, -1):
-        c_send(2, way)
-        b_first(-way)
-    keep(0, 0, pl.ds(0, BOTH))
-    a_step(0, (1,))
-    a_step(0, (3,))
-    b_second(0)
-    a_step(0, (2,))
-    for way in (1, -1):
-        c_send(3, way)
-        b_first(-2 * way)
-    a_step(1, (0,))
-    b_second(1)
-    b_second(-1)
-    a_step(1, (1,))
-    a_step(1, (3,))
-    for way in (1, -1):
-        c_send(4, way)
-        b_first(-3 * way)
-    a_step(1, (2,))
-    b_last_two(0)
-    b_second(2)
-    b_second(-2)
-    a_step(2, (0,))
-    a_step(2, (1,))
-    a_step(2, (3,))
-    for way in (1, -1):
-        c_last[4, way].wait_recv()
-    b_first(4)
-    b_last_two(1)
-    b_last_two(-1)
-    a_step(2, (2,))
-    b_second(3)
-    b_second(-3)
-    a_step(3, (0,))
-    b_last_two(2)
-    b_last_two(-2)
-    a_step(3, (1, 3, 2))
-    b_second(4)
-    a_step(4, (0, 1, 3, 2))
-    b_last_two(3)
-    b_last_two(-3)
-    b_last_two(4)
+    steps = {
+        "a_first": a_first, "a": a_step, "a_end": a_end, "c": c_step,
+        "first": b_first, "second": b_second, "end": b_end,
+    }
+    for i, (name, *which) in enumerate(GATHER_ORDER):
+        steps[name](*which)
+        if i == 7:
+            keep(0, 0, pl.ds(0, BOTH))
 
 
 def split(value):
@@ -534,7 +512,7 @@
     lane = lax.broadcasted_iota(jnp.int32, (W, W), 1)
     z, y = tile_place()
 
-    def extract_one(dz, dy):
+    def cut(dz, dy):
         p = turned(z, dz, NZ) * NY + turned(y, dy, NY)
         start = jnp.clip(rows[p] - top, -W, TS) + W
         column = jnp.clip(cols[p] - left, -W, TS) + W
@@ -550,10 +528,6 @@
                 if kind == m:
                     ext[spot(dz, dy), rows_in] = moved[rows_of]
 
-    def extract(offset):
-        for dy in range(NY):
-            extract_one(offset, dy)
-
     def ready():
         pl.semaphore_wait(barrier, len(greeted) + jnp.where(d == 0, DEPTH - 1, 1))
         for load in loads[9:]:
@@ -587,7 +561,7 @@
         return put
 
     scatter(
-        extract, ready, done(0), done(1), ext, a_recv, a_side, b_recv, b_sum, c_recv, send
+        cut, ready, done(0), done(1), ext, a_recv, a_side, b_recv, b_sum, c_recv, send
     )
 
     def grad_copy(j):

time: 93.5 us -> 89.6 us (0.958)
  Pallas kernels: 92.6 us -> 88.6 us
    pallas_call x1, Pallas kernels: 88.6 us -> 84.4 us  [local(): pl.pallas_call(main_kernel, out_shape=jax.ShapeDtypeStruct((POS, BOTH, W)...]
where the time goes in v4:
time: 89.6 us; the launch traced here: 89.4 us
  Pallas kernels  88.6 us (99%)
    pallas_call x1, Pallas kernels, local(): pl.pallas_call(main_kernel, out_shape=jax.ShapeDtypeStruct((POS, BOTH, W)...  84.4 us
    pallas_call x1, Pallas kernels, local(): pl.pallas_call(deposit_kernel, out_shape=(jax.ShapeDtypeStruct((1, 1, TS,...  4.23 us

profile of v4, /device:TPU:2, one launch (start us, length us, event | category | flops | bytes accessed | tf_op | source)
XLA Modules:
  0.0 89.4 jit_solution(11600131748204631160)
XLA Ops:
  0.6 84.4 %main.1.grads = f32[32,256,128]{2,1,0:T(8,128)} custom-call(s32[32]{0:T(128)} %rows.1, s32[32]{0:T(128)} %cols.1, s32[32]{0:T(128)} %slots.1, f32[1,1,384,384]{3,2,1,0:T(8,128)} %phase.1, f32[1,1,384,384]{3,2,1,0:T(8,128)} %absorb.1, f32[2,4,128,128]{3,2,1,0:T(8,128)} %probe_hbm.1, s32[1,128,128]{2,1,0:T(8,128)} %counts_hbm.1, ...), custom_call_target="tpu_custom_call" | custom-call | tf_op jit(solution)/shard_map/main/pallas_call | solution.py:647
  85.0 4.2 %deposit.1 = (f32[1,1,384,384]{3,2,1,0:T(8,128)}, f32[1,1,384,384]{3,2,1,0:T(8,128)}) custom-call(s32[32]{0:T(128)} %rows.1, s32[32]{0:T(128)} %cols.1, s32[32]{0:T(128)} %slots.1, f32[32,256,128]{2,1,0:T(8,128)} %main.1.grads), custom_call_target="tpu_custom_call" | custom-call | tf_op jit(solution)/shard_map/deposit/pallas_call | solution.py:687

commit v5 on v4

--- a/solution.py
+++ b/solution.py
@@ -76,51 +76,47 @@
     return dr, dc, (dr > -W) & (dr < TS) & (dc > -W) & (dc < TS)
 
 
-def deposit_kernel(rows, cols, slots, grads, phase_out, absorb_out, acc, held, sems):
+def deposit_kernel(rows, cols, slots, grads, phase_out, absorb_out, acc, found, sems):
     me = lax.axis_index("tile")
     top, left = tile_corner(slots, me)
-
     z, y = tile_place()
-
-    def fetch(p):
-        row = lax.shift_right_logical(p, 2)
-        place = turned(row, -z, NZ) * NY + turned(p - row * NY, -y, NY)
-        return pltpu.make_async_copy(grads.at[place], held.at[p], sems.at[p])
-
-    def begin(p, carry):
+    lane = lax.broadcasted_iota(jnp.int32, (W, W), 1)
+
+    def look(p, count):
+        found[count] = p
         dr, dc, touches = overlap(rows, cols, p, top, left)
-
-        @pl.when(touches)
-        def _():
-            fetch(p).start()
-
-        return carry
-
-    lax.fori_loop(0, POS, begin, 0)
-    acc[...] = jnp.zeros_like(acc)
-    lane = lax.broadcasted_iota(jnp.int32, (W, W), 1)
-
-    def one(p, carry):
-        dr, dc, touches = overlap(rows, cols, p, top, left)
-
-        @pl.when(touches)
-        def _():
-            fetch(p).wait()
-            start = dr + W
-            chunk = lax.shift_right_logical(dc + W, 7)
-            shift = dc + W - chunk * W
-            for m in range(2):
-                pieces = [held[p, rows_in] for rows_in, kind, _ in BANDS if kind == m]
-                moved = pltpu.roll(jnp.concatenate(pieces, 0), shift, 1)
-                acc[m, chunk, pl.ds(start, W), :] += jnp.where(lane >= shift, moved, 0.0)
-                acc[m, chunk + 1, pl.ds(start, W), :] += jnp.where(lane < shift, moved, 0.0)
-
-        return carry
-
-    lax.fori_loop(0, POS, one, 0)
+        return count + jnp.where(touches, 1, 0)
+
+    count = lax.fori_loop(0, POS, look, jnp.int32(0))
+    copies = []
     for m, target in enumerate((phase_out, absorb_out)):
+        acc[m, 1 : CHUNKS - 1, W : W + TS] = jnp.zeros((CHUNKS - 2, TS, W), jnp.float32)
+
+        def one(i, carry, m=m):
+            p = found[i]
+            row = lax.shift_right_logical(p, 2)
+            place = turned(row, -z, NZ) * NY + turned(p - row * NY, -y, NY)
+            start = rows[p] - top + W
+            column = cols[p] - left + W
+            chunk = lax.shift_right_logical(column, 7)
+            shift = column - chunk * W
+            pieces = [grads[place, rows_in] for rows_in, kind, _ in BANDS if kind == m]
+            moved = pltpu.roll(jnp.concatenate(pieces, 0), shift, 1)
+            acc[m, chunk, pl.ds(start, W), :] += jnp.where(lane >= shift, moved, 0.0)
+            acc[m, chunk + 1, pl.ds(start, W), :] += jnp.where(lane < shift, moved, 0.0)
+            return carry
+
+        lax.fori_loop(0, count, one, 0)
         for c in range(TS // W):
-            target[0, 0, :, c * W : (c + 1) * W] = acc[m, c + 1, W : W + TS, :]
+            copy = pltpu.make_async_copy(
+                acc.at[m, c + 1, pl.ds(W, TS)],
+                target.at[0, 0, :, pl.ds(c * W, W)],
+                sems.at[len(copies)],
+            )
+            copy.start()
+            copies.append(copy)
+    for copy in copies:
+        copy.wait()
 
 
 def tile_place():
@@ -329,7 +325,7 @@
         steps[name](*which)
 
 
-def gather(held, keep, send):
+def gather(held, send):
     arrivals = Arrivals()
 
     def z_copy(dz, dy, part, way):
@@ -348,15 +344,12 @@
         if s > 0:
             arrivals.wait(("a", stream, way, s - 1))
         elif stream > 0:
-            fresh = arrivals.wait(("side", stream))
+            arrivals.wait(("side", stream))
         arrivals["a", stream, way, s] = z_copy(-way * s, -stream, PART_A, way)
-        if s > 0 or (stream > 0 and fresh):
-            keep(-way * s, -stream, PART_A)
 
     def a_end(stream, way):
         hops = HOPS[stream, way]
         arrivals.wait(("a", stream, way, hops - 1))
-        keep(-way * hops, -stream, PART_A)
 
     def c_step(away, way):
         part = pl.ds(ROWS_A + half_of(way), HALF_B) if away == 4 else PART_B
@@ -372,30 +365,23 @@
             arrivals.wait(("c", abs(offset), 1 if offset < 0 else -1))
         for way in (1, -1):
             arrivals["b", offset, way] = y_copy(offset, 0, PART_B, way)
-        if offset != 0:
-            keep(offset, 0, PART_B)
 
     def b_second(offset):
         way = 1 if offset % 2 == 0 else -1
         arrivals.wait(("b", offset, way))
         arrivals["b", offset, 2] = y_copy(offset, -way, PART_B, way)
-        keep(offset, -way, PART_B)
 
     def b_end(offset):
         way = 1 if offset % 2 == 0 else -1
         arrivals.wait(("b", offset, -way))
-        keep(offset, way, PART_B)
         arrivals.wait(("b", offset, 2))
-        keep(offset, 2, PART_B)
 
     steps = {
         "a_first": a_first, "a": a_step, "a_end": a_end, "c": c_step,
         "first": b_first, "second": b_second, "end": b_end,
     }
-    for i, (name, *which) in enumerate(GATHER_ORDER):
+    for name, *which in GATHER_ORDER:
         steps[name](*which)
-        if i == 7:
-            keep(0, 0, pl.ds(0, BOTH))
 
 
 def split(value):
@@ -428,7 +414,7 @@
 STEP, STEP_BACK, DFT, DFT_BACK = (0, 1), (1, 0), (2, 3), (3, 2)
 
 
-def chain(trans, trans_ready, probe, counts, tables, waves, grads, grad_done):
+def chain(trans, trans_ready, probe, counts, tables, waves, grads, own, grad_done):
     fields = [(probe[0, m], probe[1, m]) for m in range(MODES)]
     for j in range(DEPTH):
         trans_ready(j)
@@ -454,18 +440,19 @@
             absorb_part = absorb_part - (wr * real + wi * imag)
             leaving.append((real, imag))
         fields = leaving
+        target = grads.at[j] if j > 0 else own
         for rows_in, kind, rows_of in BANDS:
-            grads[j, rows_in] = (phase_part, absorb_part)[kind][rows_of]
+            target[rows_in] = (phase_part, absorb_part)[kind][rows_of]
         grad_done(j)
 
 
 def main_kernel(
     rows_hbm, cols_hbm, slots_hbm, phase, absorb, probe_hbm, counts_hbm, tables_hbm,
-    out,
+    held,
     rows, cols, slots, probe, counts, tables,
-    padded, ext, a_recv, a_side, b_recv, b_sum, c_recv, held,
-    trans, waves, grads, got,
-    load_sems, s_send, s_recv, g_send, g_recv, t_send, t_recv, d_send, d_recv, keep_sems,
+    padded, ext, a_recv, a_side, b_recv, b_sum, c_recv,
+    trans, waves, grads,
+    load_sems, s_send, s_recv, g_send, g_recv, t_send, t_recv, d_send, d_recv,
 ):
     me = lax.axis_index("tile")
     d = lax.axis_index("depth")
@@ -567,7 +554,7 @@
     def grad_copy(j):
         return pltpu.make_async_remote_copy(
             src_ref=grads.at[j],
-            dst_ref=got,
+            dst_ref=held.at[0],
             send_sem=d_send.at[j],
             recv_sem=d_recv.at[0],
             device_id={"depth": j},
@@ -594,10 +581,8 @@
         def grad_done(j):
             if j > 0:
                 grad_copy(j).start()
-            else:
-                held[0] = grads[0]
-
-        chain(trans, trans_ready, probe, counts, tables, waves, grads, grad_done)
+
+        chain(trans, trans_ready, probe, counts, tables, waves, grads, held.at[0], grad_done)
 
     @pl.when(d != 0)
     def _():
@@ -606,27 +591,16 @@
         for part in range(2):
             trans_copy(d, part).wait_send()
         pltpu.make_async_remote_copy(
-            src_ref=got,
-            dst_ref=got,
+            src_ref=held.at[0],
+            dst_ref=held.at[0],
             send_sem=d_send.at[0],
             recv_sem=d_recv.at[0],
             device_id={"depth": 0},
             device_id_type=MESH,
         ).wait_recv()
-        held[0] = got[...]
 
     send_back = Sender(g_send, g_recv)
-    kept = []
-
-    def keep(dz, dy, part):
-        place = spot(dz, dy)
-        copy = pltpu.make_async_copy(
-            held.at[place, part], out.at[place, part], keep_sems.at[len(kept)]
-        )
-        copy.start()
-        kept.append(copy)
-
-    gather(held, keep, send_back)
+    gather(held, send_back)
 
     @pl.when(d == 0)
     def _():
@@ -635,8 +609,6 @@
 
     send.finish()
     send_back.finish()
-    for copy in kept:
-        copy.wait()
 
 
 def local(phase, absorb, probe, row_offsets, col_offsets, tile_slot, counts):
@@ -648,7 +620,7 @@
         main_kernel,
         out_shape=jax.ShapeDtypeStruct((POS, BOTH, W), f32),
         in_specs=[HBM] * 8,
-        out_specs=HBM,
+        out_specs=VMEM,
         scratch_shapes=[
             pltpu.SMEM((POS,), jnp.int32),
             pltpu.SMEM((POS,), jnp.int32),
@@ -663,11 +635,9 @@
             pltpu.VMEM((24, ROWS_B, W), f32),
             pltpu.VMEM((NZ, ROWS_B, W), f32),
             pltpu.VMEM((8, ROWS_B, W), f32),
-            pltpu.VMEM((POS, BOTH, W), f32),
             pltpu.VMEM((DEPTH, 2, W, W), f32),
             pltpu.VMEM((DEPTH, MODES, 2, W, W), f32),
             pltpu.VMEM((DEPTH, BOTH, W), f32),
-            pltpu.VMEM((BOTH, W), f32),
             dma((12,)),
             dma((SCATTER_COPIES,)),
             dma((SCATTER_COPIES,)),
@@ -677,24 +647,26 @@
             dma((2, DEPTH)),
             dma((DEPTH,)),
             dma((1,)),
-            dma((2 * POS,)),
         ],
         compiler_params=pltpu.CompilerParams(
-            collective_id=0, has_side_effects=True, vmem_limit_bytes=60 * mib
+            collective_id=0, has_side_effects=True, vmem_limit_bytes=40 * mib
         ),
         name="main",
-    )(row_offsets, col_offsets, tile_slot, phase, absorb, probe, counts, tables)
+    )(*(
+        pltpu.with_memory_space_constraint(v, pltpu.HBM)
+        for v in (row_offsets, col_offsets, tile_slot, phase, absorb, probe, counts, tables)
+    ))
     return pl.pallas_call(
         deposit_kernel,
         out_shape=(jax.ShapeDtypeStruct((1, 1, TS, TS), f32),) * 2,
-        in_specs=[SMEM, SMEM, SMEM, ANY],
-        out_specs=(VMEM, VMEM),
+        in_specs=[SMEM, SMEM, SMEM, VMEM],
+        out_specs=(HBM, HBM),
         scratch_shapes=[
-            pltpu.VMEM((2, TS // W + 2, PADDED, W), f32),
-            pltpu.VMEM((POS, BOTH, W), f32),
-            dma((POS,)),
+            pltpu.VMEM((2, CHUNKS, PADDED, W), f32),
+            pltpu.SMEM((POS,), jnp.int32),
+            dma((2 * (CHUNKS - 2),)),
         ],
-        compiler_params=pltpu.CompilerParams(vmem_limit_bytes=60 * mib),
+        compiler_params=pltpu.CompilerParams(vmem_limit_bytes=24 * mib),
         name="deposit",
     )(row_offsets, col_offsets, tile_slot, gathered)
 

time: 89.6 us -> 87.2 us (0.973)
  Pallas kernels: 88.6 us -> 85.8 us
    pallas_call x1, Pallas kernels: 4.23 us -> 2.48 us  [local(): pl.pallas_call(deposit_kernel, out_shape=(jax.ShapeDtypeStruct((1, 1, TS,...]
    pallas_call x1, Pallas kernels: 84.4 us -> 83.3 us  [local(): pl.pallas_call(main_kernel, out_shape=jax.ShapeDtypeStruct((POS, BOTH, W)...]
where the time goes in v5:
time: 87.2 us; the launch traced here: 86.7 us
  Pallas kernels  85.8 us (98%)
    pallas_call x1, Pallas kernels, local(): pl.pallas_call(main_kernel, out_shape=jax.ShapeDtypeStruct((POS, BOTH, W)...  83.3 us
    pallas_call x1, Pallas kernels, local(): pl.pallas_call(deposit_kernel, out_shape=(jax.ShapeDtypeStruct((1, 1, TS,...  2.48 us

profile of v5, /device:TPU:2, one launch (start us, length us, event | category | flops | bytes accessed | tf_op | source)
XLA Modules:
  0.0 86.7 jit_solution(7211244166971699016)
XLA Ops:
  0.6 0.0 copy-start.2
  0.6 0.0 copy-start.1
  0.7 0.0 copy-start
  0.7 83.3 %main.1.grads = f32[32,256,128]{2,1,0:T(8,128)S(1)} custom-call(s32[32]{0:T(128)} %rows.1, s32[32]{0:T(128)} %cols.1, s32[32]{0:T(128)} %slots.1, f32[1,1,384,384]{3,2,1,0:T(8,128)} %phase.1, f32[1,1,384,384]{3,2,1,0:T(8,128)} %absorb.1, f32[2,4,128,128]{3,2,1,0:T(8,128)} %probe_hbm.1, s32[1,128,128]{2,1,0:T(8,128)} %counts_hbm.1, ...), custom_call_target="tpu_custom_call" | custom-call | tf_op jit(solution)/shard_map/main/pallas_call | solution.py:619
  84.0 0.0 copy-done.2
  84.0 0.0 copy-done.1
  84.0 0.0 copy-done
  84.0 2.5 %deposit.1 = (f32[1,1,384,384]{3,2,1,0:T(8,128)}, f32[1,1,384,384]{3,2,1,0:T(8,128)}) custom-call(s32[32]{0:T(128)S(1)} %copy-done, s32[32]{0:T(128)S(1)} %copy-done.1, s32[32]{0:T(128)S(1)} %copy-done.2, f32[32,256,128]{2,1,0:T(8,128)S(1)} %main.1.grads), custom_call_target="tpu_custom_call" | custom-call | tf_op jit(solution)/shard_map/deposit/pallas_call | solution.py:659
Async XLA Ops:
  0.6 83.3 %copy-start.2 = (s32[32]{0:T(128)S(1)}, s32[32]{0:T(128)}, u32[]{:S(2)}) copy-start(s32[32]{0:T(128)} %slots.1) | copy-start | bytes 388
  0.6 83.3 %copy-start.1 = (s32[32]{0:T(128)S(1)}, s32[32]{0:T(128)}, u32[]{:S(2)}) copy-start(s32[32]{0:T(128)} %cols.1) | copy-start | bytes 388
  0.7 83.3 %copy-start = (s32[32]{0:T(128)S(1)}, s32[32]{0:T(128)}, u32[]{:S(2)}) copy-start(s32[32]{0:T(128)} %rows.1) | copy-start | bytes 388

commit v6 on v5

--- a/solution.py
+++ b/solution.py
@@ -171,37 +171,37 @@
     (0, 1): 4, (1, 1): 4, (2, -1): 4, (3, -1): 4, (2, 1): 3, (3, 1): 3, (0, -1): 3, (1, -1): 3,
 }
 SCATTER_ORDER = (
-    ("cut", 4, 1), ("cut", 4, 3), ("cut", 4, 2), ("far", 4), ("cut", 3, 2), ("a", 1, 1, 0),
-    ("a", 3, -1, 0), ("cut", -1, 2), ("a", 2, 1, 0), ("cut", -3, 0), ("cut", -3, 2),
-    ("cut", 3, 1), ("a", 2, -1, 0), ("cut", -2, 3), ("cut", -3, 1), ("far", 3), ("cut", 3, 3),
-    ("cut", -2, 1), ("far", -3), ("cut", 4, 0), ("cut", -1, 0), ("a", 3, 1, 0), ("cut", -1, 3),
-    ("a", 1, -1, 0), ("cut", 3, 0), ("cut", 1, 1), ("a", 0, 1, 0), ("cut", 0, 2), ("cut", -2, 0),
-    ("a", 0, -1, 0), ("cut", -2, 2), ("near", 4), ("cut", -3, 3), ("cut", 2, 0), ("a", 1, 1, 1),
-    ("cut", 0, 1), ("cut", 2, 1), ("cut", 1, 2), ("far", -2), ("a", 2, -1, 1), ("cut", 2, 3),
-    ("cut", 0, 3), ("a", 1, -1, 1), ("near", -3), ("a", 3, 1, 1), ("a", 3, -1, 1), ("cut", 2, 2),
-    ("a", 0, -1, 1), ("a", 0, 1, 1), ("a", 1, 1, 2), ("far", 2), ("sum", 4), ("near", 3),
-    ("c", 4, 1), ("a", 2, 1, 1), ("near", -2), ("cut", -1, 1), ("a", 2, -1, 2), ("c", 4, -1),
-    ("far", -1), ("sum", -3), ("near", 2), ("a", 3, -1, 2), ("cut", 1, 3), ("a", 3, 1, 2),
-    ("cut", 0, 0), ("a", 1, -1, 2), ("far", 0), ("a", 1, 1, 3), ("c", 3, -1), ("sum", 3),
-    ("c", 3, 1), ("far", 1), ("a", 3, -1, 3), ("a", 2, 1, 2), ("near", -1), ("a", 2, -1, 3),
-    ("side", 1), ("sum", -2), ("a", 0, 1, 2), ("c", 2, -1), ("sum", 2), ("near", 1), ("c", 2, 1),
-    ("near", 0), ("side", 3), ("a", 0, -1, 2), ("sum", -1), ("cut", 1, 0), ("a", 0, 1, 3),
-    ("side", 2), ("sum", 1), ("c", 1, -1), ("c", 1, 1), ("sum", 0), ("side", 0), ("done_a",),
+    ("cut", 4, 2), ("cut", 4, 1), ("a", 1, 1, 0), ("cut", 4, 3), ("far", 4), ("cut", 2, 2),
+    ("cut", 3, 3), ("a", 3, -1, 0), ("cut", -3, 1), ("cut", -3, 2), ("cut", -1, 2),
+    ("a", 3, 1, 0), ("a", 2, -1, 0), ("cut", -3, 0), ("cut", 3, 2), ("cut", 3, 1), ("cut", -1, 1),
+    ("far", 3), ("cut", 1, 2), ("cut", 4, 0), ("cut", 1, 3), ("cut", 0, 1), ("cut", 0, 0),
+    ("a", 1, -1, 0), ("cut", -2, 1), ("far", -3), ("a", 1, 1, 1), ("cut", -3, 3), ("cut", 2, 3),
+    ("a", 0, -1, 0), ("near", 4), ("a", 0, 1, 0), ("cut", 2, 0), ("cut", -2, 2), ("cut", -2, 3),
+    ("cut", -2, 0), ("cut", 3, 0), ("a", 3, 1, 1), ("cut", 1, 1), ("a", 2, 1, 0), ("cut", 2, 1),
+    ("a", 2, -1, 1), ("far", -2), ("near", 3), ("a", 1, -1, 1), ("cut", -1, 0), ("a", 3, -1, 1),
+    ("near", -3), ("far", 2), ("a", 1, 1, 2), ("cut", 0, 2), ("a", 0, 1, 1), ("a", 0, -1, 1),
+    ("sum", 4), ("far", 1), ("c", 4, -1), ("c", 4, 1), ("a", 2, -1, 2), ("near", -2),
+    ("a", 2, 1, 1), ("a", 1, -1, 2), ("near", 2), ("a", 3, 1, 2), ("sum", 3), ("cut", -1, 3),
+    ("a", 3, -1, 2), ("far", -1), ("cut", 0, 3), ("a", 1, 1, 3), ("c", 3, 1), ("far", 0),
+    ("sum", -3), ("c", 3, -1), ("cut", 1, 0), ("sum", -2), ("near", 1), ("a", 2, -1, 3),
+    ("a", 2, 1, 2), ("a", 3, -1, 3), ("a", 0, 1, 2), ("near", -1), ("sum", 2), ("c", 2, -1),
+    ("c", 2, 1), ("side", 1), ("sum", 1), ("near", 0), ("side", 2), ("a", 0, -1, 2), ("side", 3),
+    ("a", 0, 1, 3), ("sum", -1), ("c", 1, -1), ("c", 1, 1), ("side", 0), ("sum", 0), ("done_a",),
     ("done_b",),
 )
 GATHER_ORDER = (
-    ("c", 1, 1), ("c", 1, -1), ("a_first",), ("first", 0), ("a", 0, -1, 0), ("a", 0, 1, 0),
-    ("c", 2, 1), ("first", -1), ("c", 2, -1), ("a", 2, 1, 0), ("a", 0, -1, 1), ("a", 3, -1, 0),
-    ("a", 0, 1, 1), ("first", -2), ("second", 0), ("c", 3, 1), ("a", 2, -1, 0), ("first", 2),
-    ("first", 1), ("a", 1, 1, 0), ("c", 3, -1), ("second", -1), ("a", 3, -1, 1), ("a", 2, 1, 1),
-    ("a", 3, 1, 0), ("a", 2, -1, 1), ("a", 1, -1, 0), ("a", 0, 1, 2), ("first", -3),
-    ("a", 1, 1, 1), ("a", 3, -1, 2), ("c", 4, 1), ("first", 3), ("c", 4, -1), ("a", 3, 1, 1),
-    ("a", 2, -1, 2), ("second", 1), ("second", 2), ("a", 2, 1, 2), ("end", -1), ("a", 1, -1, 1),
-    ("a", 1, 1, 2), ("first", 4), ("a", 0, -1, 2), ("second", 3), ("a", 3, 1, 2), ("a", 0, 1, 3),
-    ("second", -2), ("a", 3, -1, 3), ("a", 1, -1, 2), ("end", 2), ("end", 0), ("end", 1),
-    ("second", -3), ("a", 2, -1, 3), ("a", 1, 1, 3), ("second", 4), ("a_end", 0, 1), ("end", 3),
-    ("end", -2), ("a_end", 0, -1), ("a_end", 3, 1), ("a_end", 3, -1), ("end", -3),
-    ("a_end", 1, -1), ("a_end", 2, 1), ("a_end", 1, 1), ("end", 4), ("a_end", 2, -1),
+    ("c", 1, -1), ("c", 1, 1), ("a_first",), ("a", 0, 1, 0), ("first", 0), ("a", 0, -1, 0),
+    ("c", 2, -1), ("c", 2, 1), ("first", 1), ("a", 3, -1, 0), ("a", 1, -1, 0), ("first", -1),
+    ("a", 2, -1, 0), ("second", 0), ("a", 1, 1, 0), ("a", 2, 1, 0), ("c", 3, 1), ("first", -2),
+    ("second", 1), ("first", 2), ("a", 0, 1, 1), ("c", 3, -1), ("a", 0, -1, 1), ("a", 3, -1, 1),
+    ("a", 1, 1, 1), ("a", 3, 1, 0), ("first", -3), ("c", 4, 1), ("a", 2, -1, 1), ("a", 0, 1, 2),
+    ("second", -1), ("second", 2), ("c", 4, -1), ("a", 2, 1, 1), ("first", 3), ("end", 1),
+    ("a", 1, -1, 1), ("a", 3, 1, 1), ("a", 2, -1, 2), ("a", 3, -1, 2), ("a", 1, 1, 2),
+    ("first", 4), ("end", 0), ("a", 1, -1, 2), ("a", 0, 1, 3), ("end", -1), ("a", 2, 1, 2),
+    ("second", -2), ("second", 3), ("a", 0, -1, 2), ("a", 1, 1, 3), ("a", 3, -1, 3),
+    ("second", 4), ("second", -3), ("end", 2), ("a_end", 1, -1), ("a", 3, 1, 2), ("a", 2, -1, 3),
+    ("end", -2), ("a_end", 0, -1), ("end", 3), ("a_end", 1, 1), ("end", -3), ("a_end", 0, 1),
+    ("a_end", 3, -1), ("end", 4), ("a_end", 2, -1), ("a_end", 2, 1), ("a_end", 3, 1),
 )
 SCATTER_COPIES = 28 + 3 + 24 + 8
 GATHER_COPIES = 28 + 3 + 24 + 8

time: 87.2 us -> 86.4 us (level)
  no operation moved by 1% of the time
where the time goes in v6:
time: 86.4 us; the launch traced here: 86.3 us
  Pallas kernels  85.4 us (99%)
    pallas_call x1, Pallas kernels, local(): pl.pallas_call(main_kernel, out_shape=jax.ShapeDtypeStruct((POS, BOTH, W)...  82.8 us
    pallas_call x1, Pallas kernels, local(): pl.pallas_call(deposit_kernel, out_shape=(jax.ShapeDtypeStruct((1, 1, TS,...  2.61 us

profile of v6, /device:TPU:2, one launch (start us, length us, event | category | flops | bytes accessed | tf_op | source)
XLA Modules:
  0.0 86.3 jit_solution(6845938681502498127)
XLA Ops:
  0.6 0.0 copy-start.2
  0.6 0.0 copy-start.1
  0.7 0.0 copy-start
  0.7 82.8 %main.1.grads = f32[32,256,128]{2,1,0:T(8,128)S(1)} custom-call(s32[32]{0:T(128)} %rows.1, s32[32]{0:T(128)} %cols.1, s32[32]{0:T(128)} %slots.1, f32[1,1,384,384]{3,2,1,0:T(8,128)} %phase.1, f32[1,1,384,384]{3,2,1,0:T(8,128)} %absorb.1, f32[2,4,128,128]{3,2,1,0:T(8,128)} %probe_hbm.1, s32[1,128,128]{2,1,0:T(8,128)} %counts_hbm.1, ...), custom_call_target="tpu_custom_call" | custom-call | tf_op jit(solution)/shard_map/main/pallas_call | solution.py:619
  83.5 0.0 copy-done.2
  83.5 0.0 copy-done.1
  83.5 0.0 copy-done
  83.5 2.6 %deposit.1 = (f32[1,1,384,384]{3,2,1,0:T(8,128)}, f32[1,1,384,384]{3,2,1,0:T(8,128)}) custom-call(s32[32]{0:T(128)S(1)} %copy-done, s32[32]{0:T(128)S(1)} %copy-done.1, s32[32]{0:T(128)S(1)} %copy-done.2, f32[32,256,128]{2,1,0:T(8,128)S(1)} %main.1.grads), custom_call_target="tpu_custom_call" | custom-call | tf_op jit(solution)/shard_map/deposit/pallas_call | solution.py:659
Async XLA Ops:
  0.6 82.8 %copy-start.2 = (s32[32]{0:T(128)S(1)}, s32[32]{0:T(128)}, u32[]{:S(2)}) copy-start(s32[32]{0:T(128)} %slots.1) | copy-start | bytes 388
  0.6 82.8 %copy-start.1 = (s32[32]{0:T(128)S(1)}, s32[32]{0:T(128)}, u32[]{:S(2)}) copy-start(s32[32]{0:T(128)} %cols.1) | copy-start | bytes 388
  0.7 82.8 %copy-start = (s32[32]{0:T(128)S(1)}, s32[32]{0:T(128)}, u32[]{:S(2)}) copy-start(s32[32]{0:T(128)} %rows.1) | copy-start | bytes 388

commit v7 on v6

--- a/solution.py
+++ b/solution.py
@@ -147,6 +147,7 @@
     def __init__(self, send_sems, recv_sems):
         self.send_sems, self.recv_sems = send_sems, recv_sems
         self.started = []
+        self.settled = 0
 
     def copy(self, source, target, device):
         n = len(self.started)
@@ -162,8 +163,13 @@
         self.started.append(copy)
         return copy
 
+    def settle(self, lag):
+        while self.settled < len(self.started) - lag:
+            self.started[self.settled].wait_send()
+            self.settled += 1
+
     def finish(self):
-        for copy in self.started:
+        for copy in self.started[self.settled :]:
             copy.wait_send()
 
 
@@ -204,6 +210,7 @@
     ("a_end", 3, -1), ("end", 4), ("a_end", 2, -1), ("a_end", 2, 1), ("a_end", 3, 1),
 )
 SCATTER_COPIES = 28 + 3 + 24 + 8
+LAG = 24
 GATHER_COPIES = 28 + 3 + 24 + 8
 PART_A = pl.ds(0, ROWS_A)
 PART_B = pl.ds(ROWS_A, ROWS_B)
@@ -323,6 +330,7 @@
             ready()
             waiting = False
         steps[name](*which)
+        send.settle(LAG)
 
 
 def gather(held, send):
@@ -382,6 +390,7 @@
     }
     for name, *which in GATHER_ORDER:
         steps[name](*which)
+        send.settle(LAG)
 
 
 def split(value):
@@ -398,10 +407,8 @@
     halves = []
     for field in fields:
         high, low = split(jnp.concatenate(field, 1))
-        halves.append(
-            mxu(high, tables[right, 0])
-            + (mxu(low, tables[right, 0]) + mxu(high, tables[right, 1]))
-        )
+        both = mxu(jnp.concatenate([high, low], 0), tables[right, 0])
+        halves.append(both[:W] + (both[W:] + mxu(high, tables[right, 1])))
     done = []
     for half in halves:
         high, low = split(jnp.concatenate([half[:, :W], half[:, W:]], 0))
@@ -409,6 +416,17 @@
         whole = both[:, :W] + (both[:, W:] + mxu(tables[left, 1], high))
         done.append((whole[:W], whole[W:]))
     return done
+
+
+def cos_sin(phase):
+    half = 0.5 * phase
+    square = half * half
+    sine, cosine = 0.0, 0.0
+    for k in reversed(range(7)):
+        cosine = cosine * square + (-1.0) ** k / math.factorial(2 * k)
+        sine = sine * square + (-1.0) ** k / math.factorial(2 * k + 1)
+    sine = sine * half
+    return 1.0 - 2.0 * sine * sine, 2.0 * sine * cosine
 
 
 STEP, STEP_BACK, DFT, DFT_BACK = (0, 1), (1, 0), (2, 3), (3, 2)
@@ -538,8 +556,9 @@
             rows_of = slice(0, PIXELS) if part == 0 else slice(PIXELS, W)
             count = total.shape[0] // 2
             damping = jnp.exp(-total[count:])
-            trans[d, 0, rows_of] = damping * jnp.cos(total[:count])
-            trans[d, 1, rows_of] = damping * jnp.sin(total[:count])
+            cosine, sine = cos_sin(total[:count])
+            trans[d, 0, rows_of] = damping * cosine
+            trans[d, 1, rows_of] = damping * sine
 
             @pl.when(d != 0)
             def _():
@@ -567,6 +586,8 @@
             load.wait()
 
         def trans_ready(j):
+            if j == 1:
+                send.finish()
             if j > 0:
                 for part in range(2):
                     pltpu.make_async_remote_copy(
@@ -588,6 +609,7 @@
     def _():
         for load in loads[9:]:
             load.wait()
+        send.finish()
         for part in range(2):
             trans_copy(d, part).wait_send()
         pltpu.make_async_remote_copy(
@@ -607,7 +629,6 @@
         for j in range(1, DEPTH):
             grad_copy(j).wait_send()
 
-    send.finish()
     send_back.finish()
 
 

time: 86.4 us -> 86.2 us (level)
  no operation moved by 1% of the time
where the time goes in v7:
time: 86.2 us; the launch traced here: 85.9 us
  Pallas kernels  85 us (99%)
    pallas_call x1, Pallas kernels, local(): pl.pallas_call(main_kernel, out_shape=jax.ShapeDtypeStruct((POS, BOTH, W)...  82.6 us
    pallas_call x1, Pallas kernels, local(): pl.pallas_call(deposit_kernel, out_shape=(jax.ShapeDtypeStruct((1, 1, TS,...  2.39 us

profile of v7, /device:TPU:2, one launch (start us, length us, event | category | flops | bytes accessed | tf_op | source)
XLA Modules:
  0.0 85.9 jit_solution(7749585632876065407)
XLA Ops:
  0.6 0.0 copy-start.2
  0.6 0.0 copy-start.1
  0.7 0.0 copy-start
  0.7 82.6 %main.1.grads = f32[32,256,128]{2,1,0:T(8,128)S(1)} custom-call(s32[32]{0:T(128)} %rows.1, s32[32]{0:T(128)} %cols.1, s32[32]{0:T(128)} %slots.1, f32[1,1,384,384]{3,2,1,0:T(8,128)} %phase.1, f32[1,1,384,384]{3,2,1,0:T(8,128)} %absorb.1, f32[2,4,128,128]{3,2,1,0:T(8,128)} %probe_hbm.1, s32[1,128,128]{2,1,0:T(8,128)} %counts_hbm.1, ...), custom_call_target="tpu_custom_call" | custom-call | tf_op jit(solution)/shard_map/main/pallas_call | solution.py:640
  83.3 0.0 copy-done.2
  83.3 0.0 copy-done.1
  83.3 0.0 copy-done
  83.3 2.4 %deposit.1 = (f32[1,1,384,384]{3,2,1,0:T(8,128)}, f32[1,1,384,384]{3,2,1,0:T(8,128)}) custom-call(s32[32]{0:T(128)S(1)} %copy-done, s32[32]{0:T(128)S(1)} %copy-done.1, s32[32]{0:T(128)S(1)} %copy-done.2, f32[32,256,128]{2,1,0:T(8,128)S(1)} %main.1.grads), custom_call_target="tpu_custom_call" | custom-call | tf_op jit(solution)/shard_map/deposit/pallas_call | solution.py:680
Async XLA Ops:
  0.6 82.7 %copy-start.2 = (s32[32]{0:T(128)S(1)}, s32[32]{0:T(128)}, u32[]{:S(2)}) copy-start(s32[32]{0:T(128)} %slots.1) | copy-start | bytes 388
  0.6 82.7 %copy-start.1 = (s32[32]{0:T(128)S(1)}, s32[32]{0:T(128)}, u32[]{:S(2)}) copy-start(s32[32]{0:T(128)} %cols.1) | copy-start | bytes 388
  0.7 82.7 %copy-start = (s32[32]{0:T(128)S(1)}, s32[32]{0:T(128)}, u32[]{:S(2)}) copy-start(s32[32]{0:T(128)} %rows.1) | copy-start | bytes 388
